TPU v7x, 128 devices: a whole 4x4x4 slice. The times are simulated.
128 devices in a mesh: band: 4 (over z_hi, core), fft: 32 (over z_lo, x, y).
Axes of the slice: x: 4, y: 4, z: 4 (z_hi: 2, z_lo: 2; z = z_hi * 2 + z_lo), core: 2. Of those that a mesh axis runs over, the one named last changes fastest.
Arguments:
- basis: bfloat16 [512, 512, 128], P('band', 'fft'), may hold values from -6 to 6
- potential: float32 [192, 192, 192], P('fft'), may hold values from -24 to 24
- colmap: int32 [512], replicated, may hold values from 0 to 36863, as said below
- hsub_old: float32 [512, 504], P('band'), may hold values from -6 to 6
- inv_factor: float32 [512, 512], replicated, may hold values from -1 to 1.5, as said below
- angles: float32 [30, 8, 32], replicated, may hold values from -3.140625 to 3.140625
Outputs:
- hblock: bfloat16 [8, 512, 128], P('band', 'fft')
- rotated: float32 [512, 512], P(('band', 'fft'))
- bands_new: bfloat16 [8, 512, 128], P('band', 'fft')
Inputs may be any that keep to these rules, and one draw needn't show every extreme that they name: `colmap`: distinct plane positions ix * 192 + iy, one for each pencil column. `inv_factor`: zero above the diagonal, positive on it.
All inputs are finite; a program needn't handle non-finite values.
Results may differ from a plain program's by a relative error of at most 0.015.
Values may be sent and summed in bfloat16 or wider, within the bound.
A program may use at most 448 MiB of HBM per device.

v0:
```python
import functools
import math

import jax
import jax.numpy as jnp
import numpy as np
from jax import lax
from jax.experimental import pallas as pl
from jax.experimental.pallas import tpu as pltpu
from jax.sharding import PartitionSpec as P

NG = 192
NZC = 64
ORDER = 512
GROUP = 128
NCOL = 512
NBAND = 4
NFFT = 32
SLAB = 6
ROUNDS = 30
TILE = 32
F32 = jnp.float32
BF16 = jnp.bfloat16
HIGH = lax.Precision.HIGHEST
MESH = pl.DeviceIdType.MESH
NT = (((1,), (1,)), ((), ()))


def dot(a, b, precision=None):
    return jnp.dot(a, b, precision=precision, preferred_element_type=F32)


def dot_nt(a, b, precision=None):
    return lax.dot_general(a, b, NT, precision=precision, preferred_element_type=F32)


def z_table():
    slot = np.arange(NZC)
    freq = np.where(slot < NZC // 2, slot, slot - NZC) % NG
    table = np.zeros((NFFT, 8, 4, NZC), np.float64)
    z = np.arange(NG).reshape(NFFT, SLAB)
    angle = 2.0 * np.pi * ((z[:, :, None] * freq) % NG) / NG
    table[:, :SLAB, 0] = np.cos(angle)
    table[:, :SLAB, 1] = -np.sin(angle)
    table[:, :SLAB, 2] = np.sin(angle)
    table[:, :SLAB, 3] = np.cos(angle)
    return table.reshape(NFFT * 8, 4 * NZC)


def plane_angles():
    ids = np.arange(NG)
    return 2.0 * np.pi * ((ids[:, None] * ids[None, :]) % NG) / NG


def x_table():
    angle = plane_angles()
    both = np.concatenate([np.cos(angle), np.sin(angle)], 0)
    high = np.asarray(both, np.float32).astype(BF16)
    low = (both - high.astype(np.float64)).astype(BF16)
    table = np.zeros((2 * NG, 512), BF16)
    table[:, :NG] = high
    table[:, 256 : 256 + NG] = low
    return table


def y_table_left():
    angle = plane_angles()
    table = np.zeros((2, 256, 2, 256), np.float64)
    table[0, :NG, 0, :NG] = np.cos(angle)
    table[0, :NG, 1, :NG] = -np.sin(angle)
    table[1, :NG, 0, :NG] = np.sin(angle)
    table[1, :NG, 1, :NG] = np.cos(angle)
    return table.reshape(512, 512)


def seats(turn):
    return [0] + [1 + ((m - 1 + turn) % 15) for m in range(1, 16)]


def rounds(state, cos_t, sin_t, forward):
    order = range(ROUNDS) if forward else range(ROUNDS - 1, -1, -1)
    for r in order:
        seat = seats(r % 15)
        shift = r % TILE
        for m in range(8):
            first = pl.ds(TILE * seat[m], TILE)
            second = pl.ds(TILE * seat[15 - m], TILE)
            q = r * 8 + m
            c = jnp.broadcast_to(cos_t[:, q : q + 1], (TILE, 128))
            s = jnp.broadcast_to(sin_t[:, q : q + 1], (TILE, 128))
            a = state[first, :]
            b = state[second, :]
            if shift:
                b = pltpu.roll(b, TILE - shift, 0)
            if forward:
                new_a = c * a - s * b
                new_b = s * a + c * b
            else:
                new_a = c * a + s * b
                new_b = c * b - s * a
            if shift:
                new_b = pltpu.roll(new_b, shift, 0)
            state[first, :] = new_a
            state[second, :] = new_b


def rotation_kernel(
    ids, angles, inv, hsub, basis, y_out, rows_out, bands_out, state, cos_t, sin_t, y_buf, z_buf, w_buf
):
    band = ids[0]
    me = ids[1]
    ang = jnp.concatenate([angles[...], jnp.zeros((16, TILE), F32)], 0)
    ang = jnp.concatenate([ang, jnp.zeros((256, 128 - TILE), F32)], 1)
    cos_t[...] = jnp.cos(ang).T[:TILE]
    sin_t[...] = jnp.sin(ang).T[:TILE]
    row = lax.broadcasted_iota(jnp.int32, (ORDER, 128), 0)
    lane = lax.broadcasted_iota(jnp.int32, (ORDER, 128), 1)
    target = ((lane >> 3) * NFFT + me) * 4 + (lane & 7)
    target = jnp.where((lane < 32) & ((lane & 7) < 4), target, -1)
    target = jnp.where((lane >= 32) & (lane < 40), lane - 32, target)
    state[...] = (row == target).astype(F32)
    rounds(state, cos_t, sin_t, False)
    low = inv[...].astype(BF16)
    y_all = dot(state[...].T.astype(BF16), low)
    y_buf[...] = y_all
    y_own = y_buf[:, pl.ds(pl.multiple_of(band * GROUP, GROUP), GROUP)]
    y_out[...] = y_own[:40]
    z_old = dot(y_own[:32].astype(BF16), hsub[...].astype(BF16))
    z_buf[...] = jnp.zeros_like(z_buf)
    for b in range(NBAND):
        z_buf[0:32, b * GROUP : b * GROUP + 126] = z_old[:, b * 126 : (b + 1) * 126]
    pick_row = lax.broadcasted_iota(jnp.int32, (8, ORDER), 0)
    pick_lane = lax.broadcasted_iota(jnp.int32, (8, ORDER), 1)
    z_buf[32:40, :] = (pick_lane == (pick_row >> 1) * GROUP + 126 + (pick_row & 1)).astype(F32)
    state[...] = dot(low, z_buf[...].T.astype(BF16))
    rounds(state, cos_t, sin_t, True)
    rows_out[...] = state[...].T[:40]
    weights = y_own[32:40].astype(BF16)
    spread_row = lax.broadcasted_iota(jnp.int32, (GROUP, 2048), 0)
    spread_lane = lax.broadcasted_iota(jnp.int32, (GROUP, 2048), 1)
    spread = (spread_row == (spread_lane >> 4)).astype(F32).astype(BF16)
    wide = dot(weights, spread)
    own_row = lax.broadcasted_iota(jnp.int32, (16, 2048), 0)
    own_lane = lax.broadcasted_iota(jnp.int32, (16, 2048), 1)
    keep = own_row == (own_lane & 15)
    for k in range(8):
        w_buf[16 * k : 16 * k + 16, :] = jnp.where(keep, wide[k : k + 1], 0.0).astype(BF16)
    bands_out[...] = dot(w_buf[...], basis[...]).astype(BF16)


def rotation_part(ids, angles, inv, hsub, basis):
    vmem = pl.BlockSpec(memory_space=pltpu.VMEM)
    return pl.pallas_call(
        rotation_kernel,
        out_shape=(
            jax.ShapeDtypeStruct((40, GROUP), F32),
            jax.ShapeDtypeStruct((40, ORDER), F32),
            jax.ShapeDtypeStruct((128, 128), BF16),
        ),
        in_specs=[pl.BlockSpec(memory_space=pltpu.SMEM)] + [vmem] * 4,
        out_specs=(vmem,) * 3,
        scratch_shapes=[
            pltpu.VMEM((ORDER, 128), F32),
            pltpu.VMEM((TILE, 256), F32),
            pltpu.VMEM((TILE, 256), F32),
            pltpu.VMEM((128, ORDER), F32),
            pltpu.VMEM((128, ORDER), F32),
            pltpu.VMEM((128, 2048), BF16),
        ],
        compiler_params=pltpu.CompilerParams(vmem_limit_bytes=48 * 2**20),
        name="rotation_part",
    )(ids, angles, inv, hsub, basis)


def main_kernel(
    basis, potential, columns, tz, tx, ty, ty_t, y_own, rows, bands_part,
    hblock_out, rotated_out, bands_out,
    send1, recv1, send2, recv2, send3, recv3, sendh, gath, recvb, sendf, recvf,
    a_cos, a_sin, right1, right2, radius, coef, d_buf, p_buf, g_buf,
    s1, r1, s2, r2, s3, r3, sh, rh, sb, rb, sf, rf,
):
    band = lax.axis_index("band")
    me = lax.axis_index("fft")

    barrier = pltpu.get_barrier_semaphore()

    def greet(i, carry):
        pl.semaphore_signal(
            barrier, inc=1, device_id=(band, lax.rem(me + i, NFFT)), device_id_type=MESH
        )
        return carry

    lax.fori_loop(1, NFFT, greet, 0)
    for i in range(1, NBAND):
        pl.semaphore_signal(
            barrier, inc=1, device_id=(lax.rem(band + i, NBAND), me), device_id_type=MESH
        )
    pl.semaphore_wait(barrier, NFFT - 1 + NBAND - 1)

    def fft_copy(i, send, recv, ssem, rsem, whole):
        to = lax.rem(me + i, NFFT)
        return pltpu.make_async_remote_copy(
            src_ref=send if whole else send.at[to],
            dst_ref=recv.at[me],
            send_sem=ssem.at[i],
            recv_sem=rsem.at[me],
            device_id=(band, to),
            device_id_type=MESH,
        )

    def fft_arrival(i, send, recv, ssem, rsem, whole):
        source = lax.rem(me + NFFT - i, NFFT)
        return pltpu.make_async_remote_copy(
            src_ref=send if whole else send.at[source],
            dst_ref=recv.at[source],
            send_sem=ssem.at[i],
            recv_sem=rsem.at[source],
            device_id=(band, source),
            device_id_type=MESH,
        )

    def fft_start(*args):
        def step(i, carry):
            fft_copy(i, *args).start()
            return carry

        lax.fori_loop(1, NFFT, step, 0)

    def fft_wait_recv(*args):
        def step(i, carry):
            fft_arrival(i, *args).wait_recv()
            return carry

        lax.fori_loop(1, NFFT, step, 0)

    def fft_wait_send(*args):
        def step(i, carry):
            fft_copy(i, *args).wait_send()
            return carry

        lax.fori_loop(1, NFFT, step, 0)

    def band_copy(i, src, dst, ssem, rsem):
        to = lax.rem(band + i, NBAND)
        return pltpu.make_async_remote_copy(
            src_ref=src(to),
            dst_ref=dst.at[band],
            send_sem=ssem.at[i],
            recv_sem=rsem.at[band],
            device_id=(to, me),
            device_id_type=MESH,
        )

    def band_arrival(i, src, dst, ssem, rsem):
        source = lax.rem(band + NBAND - i, NBAND)
        return pltpu.make_async_remote_copy(
            src_ref=src(source),
            dst_ref=dst.at[source],
            send_sem=ssem.at[i],
            recv_sem=rsem.at[source],
            device_id=(source, me),
            device_id_type=MESH,
        )

    new = basis[2016:2048, :]
    none = jnp.zeros((16, 128), BF16)
    right = jnp.concatenate(
        [
            jnp.concatenate([new[0:16], none], 1),
            jnp.concatenate([none, new[0:16]], 1),
            jnp.concatenate([new[16:32], none], 1),
            jnp.concatenate([none, new[16:32]], 1),
            jnp.zeros((64, 256), BF16),
        ],
        0,
    )
    send1[...] = dot_nt(tz[...], right).reshape(NFFT, 8, 128)
    first = (send1, recv1, s1, r1, False)
    fft_start(*first)
    recv1[pl.ds(me, 1)] = send1[pl.ds(me, 1)]

    bands_args = (lambda to: bands_part.at[to], recvb, sb, rb)
    for i in range(1, NBAND):
        band_copy(i, *bands_args).start()
    recvb[pl.ds(band, 1)] = bands_part[pl.ds(band, 1)]

    position = columns[...].astype(F32)
    pos_x = jnp.floor((position + 0.5) * (1.0 / NG))
    pos_y = position - NG * pos_x
    k_row = lax.broadcasted_iota(jnp.int32, (256, NCOL), 0).astype(F32)
    hot_x = (k_row == pos_x).astype(F32).astype(BF16)
    hot_y = (k_row == pos_y).astype(F32).astype(BF16)
    a_both = dot(tx[...], jnp.concatenate([hot_x, hot_x], 0))
    a_cos[...] = a_both[:NG]
    a_sin[...] = a_both[NG:]
    right2[:, :NCOL] = dot(ty[:, :256], hot_y).astype(BF16)
    right2[:, NCOL:] = dot(ty[:, 256:], hot_y).astype(BF16)
    wide_y = jnp.broadcast_to(pos_y, (128, NCOL)).T
    lane_k = lax.broadcasted_iota(jnp.int32, (NCOL, 128), 1).astype(F32)
    hot_yt = jnp.concatenate(
        [(wide_y == lane_k).astype(F32), (wide_y == lane_k + 128.0).astype(F32)], 1
    ).astype(BF16)
    right1[:NCOL, :] = dot(hot_yt, ty_t[:256, :]).astype(BF16)
    right1[NCOL:, :] = dot(hot_yt, ty_t[256:, :]).astype(BF16)
    freq_x = jnp.where(pos_x < NG // 2, pos_x, pos_x - NG)
    freq_y = jnp.where(pos_y < NG // 2, pos_y, pos_y - NG)
    radius[...] = jnp.broadcast_to(freq_x * freq_x + freq_y * freq_y, (128, NCOL)).T
    g_buf[...] = jnp.zeros_like(g_buf)
    p_buf[...] = jnp.zeros_like(p_buf)

    fft_wait_recv(*first)

    lanes = lax.broadcasted_iota(jnp.int32, (8, 128), 1)
    for q in range(4):
        for j in range(4):
            total = jnp.zeros((8, 128), F32)
            for t in range(8):
                piece = recv1[8 * j + t]
                move = (16 * t - 16 * q) % 128
                if move:
                    piece = pltpu.roll(piece, move, 1)
                total = jnp.where((lanes >> 4) == t, piece, total)
            coef[q, :, 128 * j : 128 * j + 128] = total

    def vector(v, carry):
        for z in range(SLAB):
            c_re = coef[2 * v, z : z + 1, :]
            c_im = coef[2 * v + 1, z : z + 1, :]
            d_buf[NG * z : NG * z + NG, :NCOL] = (a_cos[...] * c_re - a_sin[...] * c_im).astype(BF16)
            d_buf[NG * z : NG * z + NG, NCOL:] = (a_sin[...] * c_re + a_cos[...] * c_im).astype(BF16)
        field = dot(d_buf[...], right1[...])
        for z in range(SLAB):
            v_z = potential[z]
            p_buf[NG * z : NG * z + NG, 0:NG] = (field[NG * z : NG * z + NG, 0:NG] * v_z).astype(BF16)
            p_buf[NG * z : NG * z + NG, 256 : 256 + NG] = (
                field[NG * z : NG * z + NG, 256 : 256 + NG] * v_z
            ).astype(BF16)
        back = dot(p_buf[...], right2[...])
        for z in range(SLAB):
            u_re = back[NG * z : NG * z + NG, :NCOL]
            u_im = back[NG * z : NG * z + NG, NCOL:]
            g_buf[2 * v, z : z + 1, :] = jnp.sum(
                a_cos[...] * u_re + a_sin[...] * u_im, axis=0, keepdims=True
            )
            g_buf[2 * v + 1, z : z + 1, :] = jnp.sum(
                a_cos[...] * u_im - a_sin[...] * u_re, axis=0, keepdims=True
            )
        return carry

    lax.fori_loop(0, 2, vector, 0)

    volume = 1.0 / float(NG) ** 3
    for p in range(NFFT):
        total = jnp.zeros((8, 128), F32)
        for q in range(4):
            piece = g_buf[q, :, 128 * (p // 8) : 128 * (p // 8) + 128]
            move = (16 * q - 16 * (p % 8)) % 128
            if move:
                piece = pltpu.roll(piece, move, 1)
            total = jnp.where((lanes >> 4) == q, piece, total)
        send2[p] = total * volume
    second = (send2, recv2, s2, r2, False)
    fft_start(*second)
    recv2[pl.ds(me, 1)] = send2[pl.ds(me, 1)]

    for i in range(1, NBAND):
        band_arrival(i, *bands_args).wait_recv()
    bands_total = recvb[0].astype(F32)
    for b in range(1, NBAND):
        bands_total = bands_total + recvb[b].astype(F32)
    bands_out[...] = bands_total.astype(BF16)

    fft_wait_recv(*second)
    slabs = recv2[...].reshape(NFFT * 8, 128).T.astype(BF16)
    local = dot(slabs, tz[...])
    slot = lax.broadcasted_iota(jnp.int32, (16, 128), 1) & (NZC - 1)
    freq_z = jnp.where(slot < NZC // 2, slot, slot - NZC).astype(F32)
    own_radius = radius[pl.ds(pl.multiple_of(me * 16, 16), 16), :]
    kinetic = (own_radius + freq_z * freq_z) / (2.0 * (NG // 4) ** 2)
    for v in range(2):
        term = local[32 * v : 32 * v + 16, :128] + local[32 * v + 16 : 32 * v + 32, 128:]
        coeffs = basis[2016 + 16 * v : 2032 + 16 * v, :].astype(F32)
        sendh[16 * v : 16 * v + 16, :] = (kinetic * coeffs + term).astype(BF16)
    gather_args = (lambda to: sendh, gath, sh, rh)
    for i in range(1, NBAND):
        band_copy(i, *gather_args).start()
    gath[pl.ds(band, 1)] = sendh[...].reshape(1, 32, 128)
    hblock_out[...] = sendh[...]
    for i in range(1, NBAND):
        band_arrival(i, *gather_args).wait_recv()

    pairs = dot_nt(basis[...], gath[...].reshape(128, 128))
    pair_row = lax.broadcasted_iota(jnp.int32, (2048, 128), 0)
    pair_lane = lax.broadcasted_iota(jnp.int32, (2048, 128), 1)
    pairs = jnp.where(((pair_row ^ pair_lane) & 15) == 0, pairs, 0.0)
    by_group = jnp.sum(pairs.reshape(GROUP, 16, 128), axis=1)
    pick_row = lax.broadcasted_iota(jnp.int32, (8, 128), 0)
    pick = (pick_row == (lanes >> 4)).astype(F32)
    send3[...] = dot_nt(pick, by_group, HIGH)
    third = (send3, recv3, s3, r3, True)
    fft_start(*third)
    recv3[pl.ds(me, 1)] = send3[...].reshape(1, 8, 128)
    fft_wait_recv(*third)
    new_columns = recv3[0]
    for p in range(1, NFFT):
        new_columns = new_columns + recv3[p]
    new_columns = new_columns * (1.0 / math.sqrt(2 * NCOL * NZC))
    z_new = dot_nt(y_own[0:32, :], new_columns, HIGH)
    total = rows[0:32, :] + dot(z_new, rows[32:40, :], HIGH)
    sendf[...] = total.reshape(NBAND, 8, ORDER)
    final_args = (lambda to: sendf.at[to], recvf, sf, rf)
    for i in range(1, NBAND):
        band_copy(i, *final_args).start()
    recvf[pl.ds(band, 1)] = sendf[pl.ds(band, 1)]

    fft_wait_send(*first)
    fft_wait_send(*second)
    fft_wait_send(*third)
    for i in range(1, NBAND):
        band_copy(i, *bands_args).wait_send()
        band_copy(i, *gather_args).wait_send()
    for i in range(1, NBAND):
        band_arrival(i, *final_args).wait_recv()
    final = recvf[0] + recvf[1] + recvf[2] + recvf[3]
    rotated_out[...] = final[0:4]
    for i in range(1, NBAND):
        band_copy(i, *final_args).wait_send()


def main_part(*operands):
    vmem = pl.BlockSpec(memory_space=pltpu.VMEM)
    dma = pltpu.SemaphoreType.DMA
    return pl.pallas_call(
        main_kernel,
        out_shape=(
            jax.ShapeDtypeStruct((32, 128), BF16),
            jax.ShapeDtypeStruct((4, ORDER), F32),
            jax.ShapeDtypeStruct((32, 128), BF16),
        ),
        in_specs=[vmem] * len(operands),
        out_specs=(vmem,) * 3,
        scratch_shapes=[
            pltpu.VMEM((NFFT, 8, 128), F32),
            pltpu.VMEM((NFFT, 8, 128), F32),
            pltpu.VMEM((NFFT, 8, 128), F32),
            pltpu.VMEM((NFFT, 8, 128), F32),
            pltpu.VMEM((8, 128), F32),
            pltpu.VMEM((NFFT, 8, 128), F32),
            pltpu.VMEM((32, 128), BF16),
            pltpu.VMEM((NBAND, 32, 128), BF16),
            pltpu.VMEM((NBAND, 32, 128), BF16),
            pltpu.VMEM((NBAND, 8, ORDER), F32),
            pltpu.VMEM((NBAND, 8, ORDER), F32),
            pltpu.VMEM((NG, NCOL), F32),
            pltpu.VMEM((NG, NCOL), F32),
            pltpu.VMEM((2 * NCOL, 512), BF16),
            pltpu.VMEM((512, 2 * NCOL), BF16),
            pltpu.VMEM((NCOL, 128), F32),
            pltpu.VMEM((4, 8, NCOL), F32),
            pltpu.VMEM((SLAB * NG, 2 * NCOL), BF16),
            pltpu.VMEM((SLAB * NG, 512), BF16),
            pltpu.VMEM((4, 8, NCOL), F32),
        ]
        + [dma((NFFT,))] * 6
        + [dma((NBAND,))] * 6,
        compiler_params=pltpu.CompilerParams(
            collective_id=0, has_side_effects=True, vmem_limit_bytes=56 * 2**20
        ),
        name="main_part",
    )(*operands)


def per_device(basis, potential, colmap, hsub_old, inv_factor, angles):
    ids = jnp.stack([lax.axis_index("band"), lax.axis_index("fft")]).astype(jnp.int32)
    flat = basis.reshape(2048, 128)
    y_own, rows, bands_part = rotation_part(ids, angles.reshape(240, TILE), inv_factor, hsub_old, flat)
    left = y_table_left()
    hblock, rotated, bands = main_part(
        flat,
        potential,
        colmap.reshape(1, NCOL),
        jnp.asarray(z_table().astype(BF16)),
        jnp.asarray(x_table()),
        jnp.asarray(left.astype(BF16)),
        jnp.asarray(left.T.astype(BF16)),
        y_own,
        rows,
        bands_part.reshape(NBAND, 32, 128),
    )
    return (hblock.reshape(2, 16, 128), rotated, bands.reshape(2, 16, 128))


def solution(mesh):
    in_specs = (P("band", "fft", None), P("fft", None, None), P(), P("band", None), P(), P())
    out_specs = (P("band", "fft", None), P(("band", "fft"), None), P("band", "fft", None))
    return jax.shard_map(
        per_device, mesh=mesh, in_specs=in_specs, out_specs=out_specs, check_vma=False
    )
```

profile of v0, /device:TPU:1, one launch (start us, length us, event | category | flops | bytes accessed | tf_op | source)
XLA Modules:
  0.0 62.6 jit_solution(10725341135363285989)
XLA Ops:
  0.6 0.1 pad_add_fusion.ids
  0.7 1.1 %copy.13.hsub = f32[128,504]{1,0:T(8,128)S(1)} copy(f32[128,504]{0,1:T(8,128)} %param.13) | data formatting | bytes 516096 | tf_op args[3]
  1.8 0.0 copy-start
  1.8 1.0 %copy-done = bf16[128,16,128]{2,1,0:T(8,128)(2,1)S(1)} copy-done((bf16[128,16,128]{2,1,0:T(8,128)(2,1)S(1)}, bf16[128,16,128]{2,1,0:T(8,128)(2,1)}, u32[]{:S(2)}) %copy-start) | copy-done | bytes 524312
  2.8 0.0 copy-start.1
  2.8 1.2 %copy-done.1 = f32[512,512]{1,0:T(8,128)S(1)} copy-done((f32[512,512]{1,0:T(8,128)S(1)}, f32[512,512]{1,0:T(8,128)}, u32[]{:S(2)}) %copy-start.1) | copy-done | bytes 1048600
  4.1 0.0 copy-start.2
  4.1 0.9 %copy-done.2 = f32[30,8,32]{2,1,0:T(8,128)S(1)} copy-done((f32[30,8,32]{2,1,0:T(8,128)S(1)}, f32[30,8,32]{2,1,0:T(8,128)}, u32[]{:S(2)}) %copy-start.2) | copy-done | bytes 30744
  5.0 7.1 %rotation_part.1 = (f32[40,128]{1,0:T(8,128)S(1)}, f32[40,512]{1,0:T(8,128)S(1)}, bf16[128,128]{1,0:T(8,128)(2,1)S(1)}) custom-call(s32[2]{0:T(128)S(1)} %pad_add_fusion.ids, f32[240,32]{1,0:T(8,128)S(1)} %bitcast.10, f32[512,512]{1,0:T(8,128)S(1)} %copy-done.1, f32[128,504]{1,0:T(8,128)S(1)} %copy.13.hsub, bf16[2048,128]{1,0:T(8,128)(2,1)S(1)} %bitcast.9), custom_call_target="tpu_custom_call" | custom-call | tf_op jit(solution)/shard_map/rotation_part/pallas_call | solution.py:153
  12.1 0.0 copy-start.3
  12.1 0.6 %copy-done.3 = f32[40,512]{1,0:T(8,128)} copy-done((f32[40,512]{1,0:T(8,128)}, f32[40,512]{1,0:T(8,128)S(1)}, u32[]{:S(2)}) %copy-start.3) | copy-done | bytes 81944
  12.8 0.0 copy-start.4
  12.8 0.6 copy-done.4
  13.4 0.0 copy-start.5
  13.4 0.6 copy-done.5
  14.0 44.7 %main_part.1 = (bf16[32,128]{1,0:T(8,128)(2,1)}, f32[4,512]{1,0:T(4,128)}, bf16[32,128]{1,0:T(8,128)(2,1)}) custom-call(bf16[2048,128]{1,0:T(8,128)(2,1)} %bitcast.8, f32[6,192,192]{2,1,0:T(8,128)} %potential.1, s32[1,512]{1,0:T(1,128)} %bitcast.14, bf16[256,256]{1,0:T(8,128)(2,1)} %constant.17.clone.tz, bf16[384,512]{1,0:T(8,128)(2,1)} %constant.18.clone.tx, ...), custom_call_target="tpu_custom_call" | custom-call | tf_op jit(solution)/shard_map/main_part/pallas_call | solution.py:433
  58.7 1.3 %copy.17 = bf16[2,16,128]{2,1,0:T(8,128)(2,1)} copy(bf16[2,16,128]{2,1,0:T(8,128)(2,1)} %bitcast.13) | data formatting | bytes 16384
  60.0 1.3 %copy.18 = f32[4,512]{1,0:T(4,128)} copy(f32[4,512]{1,0:T(4,128)} %get-tuple-element.19) | data formatting | bytes 16384
  61.3 1.3 %copy.19 = bf16[2,16,128]{2,1,0:T(8,128)(2,1)} copy(bf16[2,16,128]{2,1,0:T(8,128)(2,1)} %bitcast.12) | data formatting | bytes 16384
Async XLA Ops:
  1.8 1.0 %copy-start = (bf16[128,16,128]{2,1,0:T(8,128)(2,1)S(1)}, bf16[128,16,128]{2,1,0:T(8,128)(2,1)}, u32[]{:S(2)}) copy-start(bf16[128,16,128]{2,1,0:T(8,128)(2,1)} %param.10) | copy-start | bytes 1572868
  2.8 1.2 %copy-start.1 = (f32[512,512]{1,0:T(8,128)S(1)}, f32[512,512]{1,0:T(8,128)}, u32[]{:S(2)}) copy-start(f32[512,512]{1,0:T(8,128)} %inv.1) | copy-start | bytes 3145732
  4.1 0.9 %copy-start.2 = (f32[30,8,32]{2,1,0:T(8,128)S(1)}, f32[30,8,32]{2,1,0:T(8,128)}, u32[]{:S(2)}) copy-start(f32[30,8,32]{2,1,0:T(8,128)} %param.15) | copy-start | bytes 92164
  12.1 0.6 %copy-start.3 = (f32[40,512]{1,0:T(8,128)}, f32[40,512]{1,0:T(8,128)S(1)}, u32[]{:S(2)}) copy-start(f32[40,512]{1,0:T(8,128)S(1)} %get-tuple-element.10.rows) | copy-start | bytes 245764
  12.8 0.6 copy-start.4
  13.4 0.6 copy-start.5
where the time goes:
time: 63 us; the launch traced here: 62.6 us
  Pallas kernels  51.9 us (82%)
  local copies, waits for them, and re-layouts  9.99 us (16%)
  between operations  0.67 us (1%)
    pallas_call x1, Pallas kernels, main_part(): pl.pallas_call(main_kernel, out_shape=(jax.ShapeDtypeStruct((32, 128), BF...  44.7 us
    unnamed x16, local copies, waits for them, and re-layouts  9.99 us
    pallas_call x1, Pallas kernels, rotation_part(): pl.pallas_call(rotation_kernel, out_shape=(jax.ShapeDtypeStruct((40, GROU...  7.15 us

commit v1 on v0

--- a/solution.py
+++ b/solution.py
@@ -73,69 +73,96 @@
     return table.reshape(512, 512)
 
 
-def seats(turn):
-    return [0] + [1 + ((m - 1 + turn) % 15) for m in range(1, 16)]
-
-
-def rounds(state, cos_t, sin_t, forward):
-    order = range(ROUNDS) if forward else range(ROUNDS - 1, -1, -1)
-    for r in order:
-        seat = seats(r % 15)
-        shift = r % TILE
-        for m in range(8):
-            first = pl.ds(TILE * seat[m], TILE)
-            second = pl.ds(TILE * seat[15 - m], TILE)
-            q = r * 8 + m
-            c = jnp.broadcast_to(cos_t[:, q : q + 1], (TILE, 128))
-            s = jnp.broadcast_to(sin_t[:, q : q + 1], (TILE, 128))
-            a = state[first, :]
-            b = state[second, :]
-            if shift:
-                b = pltpu.roll(b, TILE - shift, 0)
-            if forward:
-                new_a = c * a - s * b
-                new_b = s * a + c * b
-            else:
-                new_a = c * a + s * b
-                new_b = c * b - s * a
-            if shift:
-                new_b = pltpu.roll(new_b, shift, 0)
-            state[first, :] = new_a
-            state[second, :] = new_b
-
-
-def rotation_kernel(
-    ids, angles, inv, hsub, basis, y_out, rows_out, bands_out, state, cos_t, sin_t, y_buf, z_buf, w_buf
-):
-    band = ids[0]
-    me = ids[1]
-    ang = jnp.concatenate([angles[...], jnp.zeros((16, TILE), F32)], 0)
-    ang = jnp.concatenate([ang, jnp.zeros((256, 128 - TILE), F32)], 1)
-    cos_t[...] = jnp.cos(ang).T[:TILE]
-    sin_t[...] = jnp.sin(ang).T[:TILE]
-    row = lax.broadcasted_iota(jnp.int32, (ORDER, 128), 0)
-    lane = lax.broadcasted_iota(jnp.int32, (ORDER, 128), 1)
+def tile_order(turn):
+    seat = [0] + [1 + ((m - 1 + turn) % 15) for m in range(1, 16)]
+    return seat[:8] + seat[:7:-1]
+
+
+def pair_step(state, table, r, forward):
+    src, dst = state.at[r % 2], state.at[(r + 1) % 2]
+    shift = r % TILE
+    c = table[0, 8 * r : 8 * r + 8]
+    s = table[1, 8 * r : 8 * r + 8]
+    a = src[0:8]
+    b = src[8:16]
+    if shift:
+        b = pltpu.roll(b, TILE - shift, 1)
+    if forward:
+        a, b = c * a - s * b, s * a + c * b
+    else:
+        a, b = c * a + s * b, c * b - s * a
+    if shift:
+        b = pltpu.roll(b, shift, 1)
+    if forward:
+        dst[0:1] = a[0:1]
+        dst[1:7] = a[2:8]
+        dst[7:8] = b[7:8]
+        dst[8:9] = a[1:2]
+        dst[9:16] = b[0:7]
+    elif r:
+        dst[0:1] = a[0:1]
+        dst[2:8] = a[1:7]
+        dst[15:16] = a[7:8]
+        dst[1:2] = b[0:1]
+        dst[8:15] = b[1:8]
+    else:
+        dst[0:8] = a
+        dst[8:16] = b
+
+
+def angle_tables(angles, table):
+    ang = jnp.concatenate([angles[...], jnp.zeros((240, 128 - TILE), F32)], 1)
+    ang = jnp.concatenate([ang, jnp.zeros((16, 128), F32)], 0)
+    for i, part in enumerate((jnp.cos(ang).T[:TILE], jnp.sin(ang).T[:TILE])):
+        for q in range(8 * ROUNDS):
+            table[i, q] = jnp.broadcast_to(part[:, q : q + 1], (TILE, 128))
+
+
+def rotate_back(me, state, table):
+    row = lax.broadcasted_iota(jnp.int32, (TILE, 128), 0)
+    lane = lax.broadcasted_iota(jnp.int32, (TILE, 128), 1)
     target = ((lane >> 3) * NFFT + me) * 4 + (lane & 7)
     target = jnp.where((lane < 32) & ((lane & 7) < 4), target, -1)
     target = jnp.where((lane >= 32) & (lane < 40), lane - 32, target)
-    state[...] = (row == target).astype(F32)
-    rounds(state, cos_t, sin_t, False)
-    low = inv[...].astype(BF16)
-    y_all = dot(state[...].T.astype(BF16), low)
-    y_buf[...] = y_all
-    y_own = y_buf[:, pl.ds(pl.multiple_of(band * GROUP, GROUP), GROUP)]
-    y_out[...] = y_own[:40]
-    z_old = dot(y_own[:32].astype(BF16), hsub[...].astype(BF16))
+    for p, tile in enumerate(tile_order(14)):
+        state[1, p] = (row + TILE * tile == target).astype(F32)
+    for r in range(ROUNDS - 1, -1, -1):
+        pair_step(state, table, r, False)
+
+
+def natural(state, which):
+    return jnp.concatenate([state[which, p] for p in list(range(8)) + list(range(15, 7, -1))], 0)
+
+
+def couple(band, state, inv, hsub, low, y_buf, y_own, z_buf):
+    low[...] = inv[...].astype(BF16)
+    y_buf[...] = dot(natural(state, 1).T.astype(BF16), low[...])
+    own = y_buf[:, pl.ds(pl.multiple_of(band * GROUP, GROUP), GROUP)]
+    y_own[...] = own[:40]
+    z_old = dot_nt(hsub[...].astype(BF16), own.astype(BF16))
+    lane = lax.broadcasted_iota(jnp.int32, (8, 128), 1)
+    row = lax.broadcasted_iota(jnp.int32, (8, 128), 0)
     z_buf[...] = jnp.zeros_like(z_buf)
     for b in range(NBAND):
-        z_buf[0:32, b * GROUP : b * GROUP + 126] = z_old[:, b * 126 : (b + 1) * 126]
-    pick_row = lax.broadcasted_iota(jnp.int32, (8, ORDER), 0)
-    pick_lane = lax.broadcasted_iota(jnp.int32, (8, ORDER), 1)
-    z_buf[32:40, :] = (pick_lane == (pick_row >> 1) * GROUP + 126 + (pick_row & 1)).astype(F32)
-    state[...] = dot(low, z_buf[...].T.astype(BF16))
-    rounds(state, cos_t, sin_t, True)
-    rows_out[...] = state[...].T[:40]
-    weights = y_own[32:40].astype(BF16)
+        z_buf[b * GROUP : b * GROUP + 126, :] = z_old[b * 126 : (b + 1) * 126, :]
+    lanes = lax.broadcasted_iota(jnp.int32, (ORDER, 128), 1)
+    rows = lax.broadcasted_iota(jnp.int32, (ORDER, 128), 0)
+    fresh = ((lanes - 32) >> 1) * GROUP + 126 + (lanes & 1)
+    z = jnp.where(lanes < 32, z_buf[...], 0.0)
+    z = jnp.where((lanes >= 32) & (lanes < 40) & (rows == fresh), 1.0, z)
+    w = dot(low[...], z.astype(BF16))
+    for p, tile in enumerate(tile_order(0)):
+        state[0, p] = w[TILE * tile : TILE * tile + TILE]
+
+
+def rotate_on(state, table, rows):
+    for r in range(ROUNDS):
+        pair_step(state, table, r, True)
+    rows[...] = natural(state, 0).T[:40]
+
+
+def vector_weights(basis, y_own, w_buf, bands_part):
+    weights = y_own[32:40, :].astype(BF16)
     spread_row = lax.broadcasted_iota(jnp.int32, (GROUP, 2048), 0)
     spread_lane = lax.broadcasted_iota(jnp.int32, (GROUP, 2048), 1)
     spread = (spread_row == (spread_lane >> 4)).astype(F32).astype(BF16)
@@ -145,42 +172,28 @@
     keep = own_row == (own_lane & 15)
     for k in range(8):
         w_buf[16 * k : 16 * k + 16, :] = jnp.where(keep, wide[k : k + 1], 0.0).astype(BF16)
-    bands_out[...] = dot(w_buf[...], basis[...]).astype(BF16)
-
-
-def rotation_part(ids, angles, inv, hsub, basis):
-    vmem = pl.BlockSpec(memory_space=pltpu.VMEM)
-    return pl.pallas_call(
-        rotation_kernel,
-        out_shape=(
-            jax.ShapeDtypeStruct((40, GROUP), F32),
-            jax.ShapeDtypeStruct((40, ORDER), F32),
-            jax.ShapeDtypeStruct((128, 128), BF16),
-        ),
-        in_specs=[pl.BlockSpec(memory_space=pltpu.SMEM)] + [vmem] * 4,
-        out_specs=(vmem,) * 3,
-        scratch_shapes=[
-            pltpu.VMEM((ORDER, 128), F32),
-            pltpu.VMEM((TILE, 256), F32),
-            pltpu.VMEM((TILE, 256), F32),
-            pltpu.VMEM((128, ORDER), F32),
-            pltpu.VMEM((128, ORDER), F32),
-            pltpu.VMEM((128, 2048), BF16),
-        ],
-        compiler_params=pltpu.CompilerParams(vmem_limit_bytes=48 * 2**20),
-        name="rotation_part",
-    )(ids, angles, inv, hsub, basis)
+    bands_part[...] = dot(w_buf[...], basis[...]).astype(BF16).reshape(NBAND, 32, 128)
 
 
 def main_kernel(
-    basis, potential, columns, tz, tx, ty, ty_t, y_own, rows, bands_part,
+    basis_in, columns_in, angles_in, tz_in, inv_in, hsub_in, tx_in, ty_in, ty_t_in, potential_in,
     hblock_out, rotated_out, bands_out,
+    basis, columns, angles, tz, inv, hsub, tx, ty, ty_t, potential,
+    state, table, low, y_buf, y_own, z_buf, rows, w_buf, bands_part,
     send1, recv1, send2, recv2, send3, recv3, sendh, gath, recvb, sendf, recvf,
     a_cos, a_sin, right1, right2, radius, coef, d_buf, p_buf, g_buf,
-    s1, r1, s2, r2, s3, r3, sh, rh, sb, rb, sf, rf,
+    s1, r1, s2, r2, s3, r3, sh, rh, sb, rb, sf, rf, loads,
 ):
     band = lax.axis_index("band")
     me = lax.axis_index("fft")
+
+    inputs = (
+        (basis_in, basis), (tz_in, tz), (angles_in, angles), (columns_in, columns), (tx_in, tx),
+        (ty_in, ty), (ty_t_in, ty_t), (inv_in, inv), (hsub_in, hsub), (potential_in, potential),
+    )
+    copies = [pltpu.make_async_copy(a, b, loads.at[i]) for i, (a, b) in enumerate(inputs)]
+    for copy in copies:
+        copy.start()
 
     barrier = pltpu.get_barrier_semaphore()
 
@@ -195,7 +208,6 @@
         pl.semaphore_signal(
             barrier, inc=1, device_id=(lax.rem(band + i, NBAND), me), device_id_type=MESH
         )
-    pl.semaphore_wait(barrier, NFFT - 1 + NBAND - 1)
 
     def fft_copy(i, send, recv, ssem, rsem, whole):
         to = lax.rem(me + i, NFFT)
@@ -262,6 +274,8 @@
             device_id_type=MESH,
         )
 
+    copies[0].wait()
+    copies[1].wait()
     new = basis[2016:2048, :]
     none = jnp.zeros((16, 128), BF16)
     right = jnp.concatenate(
@@ -276,14 +290,16 @@
     )
     send1[...] = dot_nt(tz[...], right).reshape(NFFT, 8, 128)
     first = (send1, recv1, s1, r1, False)
+    copies[2].wait()
+    angle_tables(angles, table)
+    pl.semaphore_wait(barrier, NFFT - 1 + NBAND - 1)
     fft_start(*first)
     recv1[pl.ds(me, 1)] = send1[pl.ds(me, 1)]
 
-    bands_args = (lambda to: bands_part.at[to], recvb, sb, rb)
-    for i in range(1, NBAND):
-        band_copy(i, *bands_args).start()
-    recvb[pl.ds(band, 1)] = bands_part[pl.ds(band, 1)]
-
+    rotate_back(me, state, table)
+
+    for i in range(3, 7):
+        copies[i].wait()
     position = columns[...].astype(F32)
     pos_x = jnp.floor((position + 0.5) * (1.0 / NG))
     pos_y = position - NG * pos_x
@@ -308,6 +324,9 @@
     g_buf[...] = jnp.zeros_like(g_buf)
     p_buf[...] = jnp.zeros_like(p_buf)
 
+    for i in range(7, 10):
+        copies[i].wait()
+    couple(band, state, inv, hsub, low, y_buf, y_own, z_buf)
     fft_wait_recv(*first)
 
     lanes = lax.broadcasted_iota(jnp.int32, (8, 128), 1)
@@ -363,12 +382,12 @@
     fft_start(*second)
     recv2[pl.ds(me, 1)] = send2[pl.ds(me, 1)]
 
-    for i in range(1, NBAND):
-        band_arrival(i, *bands_args).wait_recv()
-    bands_total = recvb[0].astype(F32)
-    for b in range(1, NBAND):
-        bands_total = bands_total + recvb[b].astype(F32)
-    bands_out[...] = bands_total.astype(BF16)
+    vector_weights(basis, y_own, w_buf, bands_part)
+    bands_args = (lambda to: bands_part.at[to], recvb, sb, rb)
+    for i in range(1, NBAND):
+        band_copy(i, *bands_args).start()
+    recvb[pl.ds(band, 1)] = bands_part[pl.ds(band, 1)]
+    rotate_on(state, table, rows)
 
     fft_wait_recv(*second)
     slabs = recv2[...].reshape(NFFT * 8, 128).T.astype(BF16)
@@ -386,6 +405,14 @@
         band_copy(i, *gather_args).start()
     gath[pl.ds(band, 1)] = sendh[...].reshape(1, 32, 128)
     hblock_out[...] = sendh[...]
+
+    for i in range(1, NBAND):
+        band_arrival(i, *bands_args).wait_recv()
+    bands_total = recvb[0].astype(F32)
+    for b in range(1, NBAND):
+        bands_total = bands_total + recvb[b].astype(F32)
+    bands_out[...] = bands_total.astype(BF16)
+
     for i in range(1, NBAND):
         band_arrival(i, *gather_args).wait_recv()
 
@@ -437,9 +464,19 @@
             jax.ShapeDtypeStruct((4, ORDER), F32),
             jax.ShapeDtypeStruct((32, 128), BF16),
         ),
-        in_specs=[vmem] * len(operands),
+        in_specs=[pl.BlockSpec(memory_space=pl.ANY)] * len(operands),
         out_specs=(vmem,) * 3,
-        scratch_shapes=[
+        scratch_shapes=[pltpu.VMEM(x.shape, x.dtype) for x in operands]
+        + [
+            pltpu.VMEM((2, 16, TILE, 128), F32),
+            pltpu.VMEM((2, 8 * ROUNDS, TILE, 128), F32),
+            pltpu.VMEM((ORDER, ORDER), BF16),
+            pltpu.VMEM((128, ORDER), F32),
+            pltpu.VMEM((40, GROUP), F32),
+            pltpu.VMEM((ORDER, 128), F32),
+            pltpu.VMEM((40, ORDER), F32),
+            pltpu.VMEM((128, 2048), BF16),
+            pltpu.VMEM((NBAND, 32, 128), BF16),
             pltpu.VMEM((NFFT, 8, 128), F32),
             pltpu.VMEM((NFFT, 8, 128), F32),
             pltpu.VMEM((NFFT, 8, 128), F32),
@@ -462,7 +499,8 @@
             pltpu.VMEM((4, 8, NCOL), F32),
         ]
         + [dma((NFFT,))] * 6
-        + [dma((NBAND,))] * 6,
+        + [dma((NBAND,))] * 6
+        + [dma((len(operands),))],
         compiler_params=pltpu.CompilerParams(
             collective_id=0, has_side_effects=True, vmem_limit_bytes=56 * 2**20
         ),
@@ -470,23 +508,45 @@
     )(*operands)
 
 
+def result_kernel(*refs):
+    sources, targets, sems = refs[:3], refs[3:6], refs[6]
+    copies = [
+        pltpu.make_async_copy(a, b, sems.at[i]) for i, (a, b) in enumerate(zip(sources, targets))
+    ]
+    for copy in copies:
+        copy.start()
+    for copy in copies:
+        copy.wait()
+
+
+def result_part(*operands):
+    anywhere = pl.BlockSpec(memory_space=pl.ANY)
+    return pl.pallas_call(
+        result_kernel,
+        out_shape=tuple(jax.ShapeDtypeStruct(x.shape, x.dtype) for x in operands),
+        in_specs=[anywhere] * 3,
+        out_specs=(anywhere,) * 3,
+        scratch_shapes=[pltpu.SemaphoreType.DMA((3,))],
+        compiler_params=pltpu.CompilerParams(vmem_limit_bytes=56 * 2**20),
+        name="result_part",
+    )(*operands)
+
+
 def per_device(basis, potential, colmap, hsub_old, inv_factor, angles):
-    ids = jnp.stack([lax.axis_index("band"), lax.axis_index("fft")]).astype(jnp.int32)
-    flat = basis.reshape(2048, 128)
-    y_own, rows, bands_part = rotation_part(ids, angles.reshape(240, TILE), inv_factor, hsub_old, flat)
     left = y_table_left()
-    hblock, rotated, bands = main_part(
-        flat,
-        potential,
+    results = main_part(
+        basis.reshape(2048, 128),
         colmap.reshape(1, NCOL),
+        angles.reshape(8 * ROUNDS, TILE),
         jnp.asarray(z_table().astype(BF16)),
+        inv_factor,
+        hsub_old.T,
         jnp.asarray(x_table()),
         jnp.asarray(left.astype(BF16)),
         jnp.asarray(left.T.astype(BF16)),
-        y_own,
-        rows,
-        bands_part.reshape(NBAND, 32, 128),
+        potential,
     )
+    hblock, rotated, bands = result_part(*results)
     return (hblock.reshape(2, 16, 128), rotated, bands.reshape(2, 16, 128))
 
 

time: 63 us -> 46.5 us (0.74)
  local copies, waits for them, and re-layouts: 9.99 us -> 0 us
  Pallas kernels: 51.9 us -> 45.8 us
    unnamed x16 -> x0, local copies, waits for them, and re-layouts: 9.99 us -> none
    pallas_call x1, Pallas kernels: 7.15 us -> 1.88 us  [result_part(): pl.pallas_call(result_kernel, out_shape=tuple((jax.ShapeDtypeStruct(x.sha...]
    pallas_call x1, Pallas kernels: 44.7 us -> 43.9 us  [main_part(): pl.pallas_call(main_kernel, out_shape=(jax.ShapeDtypeStruct((32, 128), BF...]
where the time goes in v1:
time: 46.5 us; the launch traced here: 46.4 us
  Pallas kernels  45.8 us (98%)
  between operations  0.64 us (1%)
    pallas_call x1, Pallas kernels, main_part(): pl.pallas_call(main_kernel, out_shape=(jax.ShapeDtypeStruct((32, 128), BF...  43.9 us
    pallas_call x1, Pallas kernels, result_part(): pl.pallas_call(result_kernel, out_shape=tuple((jax.ShapeDtypeStruct(x.sha...  1.88 us

profile of v1, /device:TPU:1, one launch (start us, length us, event | category | flops | bytes accessed | tf_op | source)
XLA Modules:
  0.0 46.4 jit_solution(8365823156009241562)
XLA Ops:
  0.6 43.9 %main_part.1 = (bf16[32,128]{1,0:T(8,128)(2,1)}, f32[4,512]{1,0:T(4,128)}, bf16[32,128]{1,0:T(8,128)(2,1)}) custom-call(bf16[2048,128]{1,0:T(8,128)(2,1)} %bitcast.6, s32[1,512]{1,0:T(1,128)} %bitcast.9, f32[240,32]{1,0:T(8,128)} %bitcast.8, bf16[256,256]{1,0:T(8,128)(2,1)} %constant.8.clone.tz_in, f32[512,512]{1,0:T(8,128)} %inv_in.1, f32[504,128]{1,0:T(8,128)} %bitcast.7, ...), custom_call_target="tpu_custom_call" | custom-call | tf_op jit(solution)/shard_map/main_part/pallas_call | solution.py:460
  44.6 1.9 %result_part.1 = (bf16[32,128]{1,0:T(8,128)(2,1)}, f32[4,512]{1,0:T(4,128)}, bf16[32,128]{1,0:T(8,128)(2,1)}) custom-call(bf16[32,128]{1,0:T(8,128)(2,1)} %get-tuple-element.9.refs_0_, f32[4,512]{1,0:T(4,128)} %get-tuple-element.10.refs_1_, bf16[32,128]{1,0:T(8,128)(2,1)} %get-tuple-element.11.refs_2_), custom_call_target="tpu_custom_call" | custom-call | tf_op jit(solution)/shard_map/result_part/pallas_call | solution.py:524

commit v2 on v1

--- a/solution.py
+++ b/solution.py
@@ -209,48 +209,37 @@
             barrier, inc=1, device_id=(lax.rem(band + i, NBAND), me), device_id_type=MESH
         )
 
-    def fft_copy(i, send, recv, ssem, rsem, whole):
-        to = lax.rem(me + i, NFFT)
+    def fft_start(send, recv, ssem, rsem, whole):
+        def step(i, carry):
+            to = lax.rem(me + i, NFFT)
+            pltpu.make_async_remote_copy(
+                src_ref=send if whole else send.at[to],
+                dst_ref=recv.at[me],
+                send_sem=ssem,
+                recv_sem=rsem,
+                device_id=(band, to),
+                device_id_type=MESH,
+            ).start()
+            return carry
+
+        lax.fori_loop(1, NFFT, step, 0)
+
+    def fft_all(send, recv, ssem, rsem, whole):
+        part = recv.at[pl.ds(0, NFFT - 1)]
         return pltpu.make_async_remote_copy(
-            src_ref=send if whole else send.at[to],
-            dst_ref=recv.at[me],
-            send_sem=ssem.at[i],
-            recv_sem=rsem.at[me],
-            device_id=(band, to),
+            src_ref=part,
+            dst_ref=part,
+            send_sem=ssem,
+            recv_sem=rsem,
+            device_id=(band, lax.rem(me + 1, NFFT)),
             device_id_type=MESH,
         )
 
-    def fft_arrival(i, send, recv, ssem, rsem, whole):
-        source = lax.rem(me + NFFT - i, NFFT)
-        return pltpu.make_async_remote_copy(
-            src_ref=send if whole else send.at[source],
-            dst_ref=recv.at[source],
-            send_sem=ssem.at[i],
-            recv_sem=rsem.at[source],
-            device_id=(band, source),
-            device_id_type=MESH,
-        )
-
-    def fft_start(*args):
-        def step(i, carry):
-            fft_copy(i, *args).start()
-            return carry
-
-        lax.fori_loop(1, NFFT, step, 0)
-
     def fft_wait_recv(*args):
-        def step(i, carry):
-            fft_arrival(i, *args).wait_recv()
-            return carry
-
-        lax.fori_loop(1, NFFT, step, 0)
+        fft_all(*args).wait_recv()
 
     def fft_wait_send(*args):
-        def step(i, carry):
-            fft_copy(i, *args).wait_send()
-            return carry
-
-        lax.fori_loop(1, NFFT, step, 0)
+        fft_all(*args).wait_send()
 
     def band_copy(i, src, dst, ssem, rsem):
         to = lax.rem(band + i, NBAND)
@@ -290,12 +279,12 @@
     )
     send1[...] = dot_nt(tz[...], right).reshape(NFFT, 8, 128)
     first = (send1, recv1, s1, r1, False)
-    copies[2].wait()
-    angle_tables(angles, table)
     pl.semaphore_wait(barrier, NFFT - 1 + NBAND - 1)
     fft_start(*first)
     recv1[pl.ds(me, 1)] = send1[pl.ds(me, 1)]
 
+    copies[2].wait()
+    angle_tables(angles, table)
     rotate_back(me, state, table)
 
     for i in range(3, 7):
@@ -498,7 +487,7 @@
             pltpu.VMEM((SLAB * NG, 512), BF16),
             pltpu.VMEM((4, 8, NCOL), F32),
         ]
-        + [dma((NFFT,))] * 6
+        + [dma] * 6
         + [dma((NBAND,))] * 6
         + [dma((len(operands),))],
         compiler_params=pltpu.CompilerParams(

time: 46.5 us -> 45.1 us (0.970)
  Pallas kernels: 45.8 us -> 44.3 us
    pallas_call x1, Pallas kernels: 43.9 us -> 42.5 us  [main_part(): pl.pallas_call(main_kernel, out_shape=(jax.ShapeDtypeStruct((32, 128), BF...]
where the time goes in v2:
time: 45.1 us; the launch traced here: 45 us
  Pallas kernels  44.3 us (98%)
  between operations  0.64 us (1%)
    pallas_call x1, Pallas kernels, main_part(): pl.pallas_call(main_kernel, out_shape=(jax.ShapeDtypeStruct((32, 128), BF...  42.5 us
    pallas_call x1, Pallas kernels, result_part(): pl.pallas_call(result_kernel, out_shape=tuple((jax.ShapeDtypeStruct(x.sha...  1.88 us

profile of v2, /device:TPU:1, one launch (start us, length us, event | category | flops | bytes accessed | tf_op | source)
XLA Modules:
  0.0 45.0 jit_solution(17878873776052014936)
XLA Ops:
  0.6 42.5 %main_part.1 = (bf16[32,128]{1,0:T(8,128)(2,1)}, f32[4,512]{1,0:T(4,128)}, bf16[32,128]{1,0:T(8,128)(2,1)}) custom-call(bf16[2048,128]{1,0:T(8,128)(2,1)} %bitcast.6, s32[1,512]{1,0:T(1,128)} %bitcast.9, f32[240,32]{1,0:T(8,128)} %bitcast.8, bf16[256,256]{1,0:T(8,128)(2,1)} %constant.8.clone.tz_in, f32[512,512]{1,0:T(8,128)} %inv_in.1, f32[504,128]{1,0:T(8,128)} %bitcast.7, ...), custom_call_target="tpu_custom_call" | custom-call | tf_op jit(solution)/shard_map/main_part/pallas_call | solution.py:449
  43.1 1.9 %result_part.1 = (bf16[32,128]{1,0:T(8,128)(2,1)}, f32[4,512]{1,0:T(4,128)}, bf16[32,128]{1,0:T(8,128)(2,1)}) custom-call(bf16[32,128]{1,0:T(8,128)(2,1)} %get-tuple-element.9.refs_0_, f32[4,512]{1,0:T(4,128)} %get-tuple-element.10.refs_1_, bf16[32,128]{1,0:T(8,128)(2,1)} %get-tuple-element.11.refs_2_), custom_call_target="tpu_custom_call" | custom-call | tf_op jit(solution)/shard_map/result_part/pallas_call | solution.py:513

commit v3 on v2

--- a/solution.py
+++ b/solution.py
@@ -10,6 +10,7 @@
 from jax.sharding import PartitionSpec as P
 
 NG = 192
+HALF = 96
 NZC = 64
 ORDER = 512
 GROUP = 128
@@ -47,30 +48,27 @@
     return table.reshape(NFFT * 8, 4 * NZC)
 
 
-def plane_angles():
-    ids = np.arange(NG)
-    return 2.0 * np.pi * ((ids[:, None] * ids[None, :]) % NG) / NG
+def half_angles():
+    return 2.0 * np.pi * (((2 * np.arange(HALF)[:, None] + 1) * np.arange(NG)) % (2 * NG)) / (2 * NG)
 
 
 def x_table():
-    angle = plane_angles()
+    angle = half_angles()
     both = np.concatenate([np.cos(angle), np.sin(angle)], 0)
     high = np.asarray(both, np.float32).astype(BF16)
     low = (both - high.astype(np.float64)).astype(BF16)
-    table = np.zeros((2 * NG, 512), BF16)
+    table = np.zeros((2 * HALF, 512), BF16)
     table[:, :NG] = high
     table[:, 256 : 256 + NG] = low
     return table
 
 
-def y_table_left():
-    angle = plane_angles()
-    table = np.zeros((2, 256, 2, 256), np.float64)
-    table[0, :NG, 0, :NG] = np.cos(angle)
-    table[0, :NG, 1, :NG] = -np.sin(angle)
-    table[1, :NG, 0, :NG] = np.sin(angle)
-    table[1, :NG, 1, :NG] = np.cos(angle)
-    return table.reshape(512, 512)
+def y_table():
+    angle = half_angles().T
+    table = np.zeros((256, 256), np.float64)
+    table[:NG, :HALF] = np.cos(angle)
+    table[:NG, 128 : 128 + HALF] = np.sin(angle)
+    return table
 
 
 def tile_order(turn):
@@ -175,13 +173,64 @@
     bands_part[...] = dot(w_buf[...], basis[...]).astype(BF16).reshape(NBAND, 32, 128)
 
 
+def split(value):
+    high = value.astype(BF16)
+    return high, (value - high.astype(F32)).astype(BF16)
+
+
+def fold_potential(potential, folded):
+    y_row = lax.broadcasted_iota(jnp.int32, (NG, 256), 0)
+    y_lane = lax.broadcasted_iota(jnp.int32, (NG, 256), 1)
+    wanted = jnp.where(y_lane < 128, HALF + y_lane, HALF - 1 + 128 - y_lane)
+    wanted = jnp.where((y_lane & 127) < HALF, wanted, -1)
+    order_y = (y_row == wanted).astype(F32).astype(BF16)
+    x_row = lax.broadcasted_iota(jnp.int32, (HALF, HALF), 0)
+    x_lane = lax.broadcasted_iota(jnp.int32, (HALF, HALF), 1)
+    order_x = (x_row + x_lane == HALF - 1).astype(F32).astype(BF16)
+    high, low = split(potential[...].reshape(SLAB * NG, NG))
+    value = dot(high, order_y) + dot(low, order_y)
+    for z in range(SLAB):
+        high, low = split(value[NG * z : NG * z + HALF])
+        low_side = dot(order_x, high) + dot(order_x, low)
+        high_side = value[NG * z + HALF : NG * z + NG]
+        for v in range(2):
+            folded[z, 0, v] = high_side[:, 128 * v : 128 * v + 128]
+            folded[z, 1, v] = low_side[:, 128 * v : 128 * v + 128]
+
+
+def times_potential(q, v):
+    (cc, cs), (sc, ss) = q
+
+    def add(m, n):
+        return m[0] + n[0], m[1] + n[1]
+
+    def sub(m, n):
+        return m[0] - n[0], m[1] - n[1]
+
+    def by_i(m):
+        return -m[1], m[0]
+
+    def scaled(m, w):
+        return m[0] * w, m[1] * w
+
+    e1, o1 = sub(cc, ss), by_i(add(sc, cs))
+    e2, o2 = add(cc, ss), by_i(sub(sc, cs))
+    high = scaled(add(e1, o1), v[0][0])
+    low = scaled(sub(e1, o1), v[1][1])
+    right = scaled(add(e2, o2), v[0][1])
+    left = scaled(sub(e2, o2), v[1][0])
+    s1, d1, s2, d2 = add(high, low), sub(high, low), add(right, left), sub(right, left)
+    odd_x, odd_y = add(d1, d2), sub(d1, d2)
+    return (add(s1, s2), (odd_y[1], -odd_y[0])), ((odd_x[1], -odd_x[0]), sub(s2, s1))
+
+
 def main_kernel(
     basis_in, columns_in, angles_in, tz_in, inv_in, hsub_in, tx_in, ty_in, ty_t_in, potential_in,
     hblock_out, rotated_out, bands_out,
     basis, columns, angles, tz, inv, hsub, tx, ty, ty_t, potential,
     state, table, low, y_buf, y_own, z_buf, rows, w_buf, bands_part,
     send1, recv1, send2, recv2, send3, recv3, sendh, gath, recvb, sendf, recvf,
-    a_cos, a_sin, right1, right2, radius, coef, d_buf, p_buf, g_buf,
+    a_cos, a_sin, phase, folded, right1, right2, radius, coef, d_buf, p_buf, g_buf,
     s1, r1, s2, r2, s3, r3, sh, rh, sb, rb, sf, rf, loads,
 ):
     band = lax.axis_index("band")
@@ -296,25 +345,28 @@
     hot_x = (k_row == pos_x).astype(F32).astype(BF16)
     hot_y = (k_row == pos_y).astype(F32).astype(BF16)
     a_both = dot(tx[...], jnp.concatenate([hot_x, hot_x], 0))
-    a_cos[...] = a_both[:NG]
-    a_sin[...] = a_both[NG:]
-    right2[:, :NCOL] = dot(ty[:, :256], hot_y).astype(BF16)
-    right2[:, NCOL:] = dot(ty[:, 256:], hot_y).astype(BF16)
+    a_cos[...] = a_both[:HALF]
+    a_sin[...] = a_both[HALF:]
+    right2[...] = dot(ty_t[...], hot_y).astype(BF16)
     wide_y = jnp.broadcast_to(pos_y, (128, NCOL)).T
     lane_k = lax.broadcasted_iota(jnp.int32, (NCOL, 128), 1).astype(F32)
     hot_yt = jnp.concatenate(
         [(wide_y == lane_k).astype(F32), (wide_y == lane_k + 128.0).astype(F32)], 1
     ).astype(BF16)
-    right1[:NCOL, :] = dot(hot_yt, ty_t[:256, :]).astype(BF16)
-    right1[NCOL:, :] = dot(hot_yt, ty_t[256:, :]).astype(BF16)
+    right1[...] = dot(hot_yt, ty[...]).astype(BF16)
+    turns = (pos_x + pos_y) * (NG - 1.0)
+    turns = turns - (2.0 * NG) * jnp.floor((turns + 0.5) * (0.5 / NG))
+    center = jnp.broadcast_to(turns * (math.pi / NG), (8, NCOL))
+    phase[0] = jnp.cos(center)
+    phase[1] = jnp.sin(center)
     freq_x = jnp.where(pos_x < NG // 2, pos_x, pos_x - NG)
     freq_y = jnp.where(pos_y < NG // 2, pos_y, pos_y - NG)
     radius[...] = jnp.broadcast_to(freq_x * freq_x + freq_y * freq_y, (128, NCOL)).T
     g_buf[...] = jnp.zeros_like(g_buf)
-    p_buf[...] = jnp.zeros_like(p_buf)
 
     for i in range(7, 10):
         copies[i].wait()
+    fold_potential(potential, folded)
     couple(band, state, inv, hsub, low, y_buf, y_own, z_buf)
     fft_wait_recv(*first)
 
@@ -331,28 +383,37 @@
             coef[q, :, 128 * j : 128 * j + 128] = total
 
     def vector(v, carry):
+        old_re, old_im = coef[2 * v], coef[2 * v + 1]
+        all_re = old_re * phase[0] - old_im * phase[1]
+        all_im = old_re * phase[1] + old_im * phase[0]
         for z in range(SLAB):
-            c_re = coef[2 * v, z : z + 1, :]
-            c_im = coef[2 * v + 1, z : z + 1, :]
-            d_buf[NG * z : NG * z + NG, :NCOL] = (a_cos[...] * c_re - a_sin[...] * c_im).astype(BF16)
-            d_buf[NG * z : NG * z + NG, NCOL:] = (a_sin[...] * c_re + a_cos[...] * c_im).astype(BF16)
+            for a, part in enumerate((a_cos, a_sin)):
+                for i, c in enumerate((all_re, all_im)):
+                    row = HALF * (4 * z + 2 * a + i)
+                    d_buf[row : row + HALF, :] = (part[...] * c[z : z + 1]).astype(BF16)
         field = dot(d_buf[...], right1[...])
         for z in range(SLAB):
-            v_z = potential[z]
-            p_buf[NG * z : NG * z + NG, 0:NG] = (field[NG * z : NG * z + NG, 0:NG] * v_z).astype(BF16)
-            p_buf[NG * z : NG * z + NG, 256 : 256 + NG] = (
-                field[NG * z : NG * z + NG, 256 : 256 + NG] * v_z
-            ).astype(BF16)
-        back = dot(p_buf[...], right2[...])
+            q = []
+            for a in range(2):
+                rows_a = [field[HALF * (4 * z + 2 * a + i) :][:HALF] for i in range(2)]
+                q.append([tuple(x[:, 128 * b : 128 * b + 128] for x in rows_a) for b in range(2)])
+            back = times_potential(q, [[folded[z, u, w] for w in range(2)] for u in range(2)])
+            for a in range(2):
+                for b in range(2):
+                    for i in range(2):
+                        row = HALF * (4 * z + 2 * a + i)
+                        p_buf[row : row + HALF, 128 * b : 128 * b + 128] = back[a][b][i].astype(BF16)
+        final = dot(p_buf[...], right2[...])
         for z in range(SLAB):
-            u_re = back[NG * z : NG * z + NG, :NCOL]
-            u_im = back[NG * z : NG * z + NG, NCOL:]
-            g_buf[2 * v, z : z + 1, :] = jnp.sum(
-                a_cos[...] * u_re + a_sin[...] * u_im, axis=0, keepdims=True
-            )
-            g_buf[2 * v + 1, z : z + 1, :] = jnp.sum(
-                a_cos[...] * u_im - a_sin[...] * u_re, axis=0, keepdims=True
-            )
+            for i in range(2):
+                even = final[HALF * (4 * z + i) :][:HALF]
+                odd = final[HALF * (4 * z + 2 + i) :][:HALF]
+                g_buf[2 * v + i, z : z + 1, :] = jnp.sum(
+                    a_cos[...] * even + a_sin[...] * odd, axis=0, keepdims=True
+                )
+        new_re, new_im = g_buf[2 * v], g_buf[2 * v + 1]
+        g_buf[2 * v] = new_re * phase[0] + new_im * phase[1]
+        g_buf[2 * v + 1] = new_im * phase[0] - new_re * phase[1]
         return carry
 
     lax.fori_loop(0, 2, vector, 0)
@@ -477,14 +538,16 @@
             pltpu.VMEM((NBAND, 32, 128), BF16),
             pltpu.VMEM((NBAND, 8, ORDER), F32),
             pltpu.VMEM((NBAND, 8, ORDER), F32),
-            pltpu.VMEM((NG, NCOL), F32),
-            pltpu.VMEM((NG, NCOL), F32),
-            pltpu.VMEM((2 * NCOL, 512), BF16),
-            pltpu.VMEM((512, 2 * NCOL), BF16),
+            pltpu.VMEM((HALF, NCOL), F32),
+            pltpu.VMEM((HALF, NCOL), F32),
+            pltpu.VMEM((2, 8, NCOL), F32),
+            pltpu.VMEM((SLAB, 2, 2, HALF, 128), F32),
+            pltpu.VMEM((NCOL, 256), BF16),
+            pltpu.VMEM((256, NCOL), BF16),
             pltpu.VMEM((NCOL, 128), F32),
             pltpu.VMEM((4, 8, NCOL), F32),
-            pltpu.VMEM((SLAB * NG, 2 * NCOL), BF16),
-            pltpu.VMEM((SLAB * NG, 512), BF16),
+            pltpu.VMEM((4 * SLAB * HALF, NCOL), BF16),
+            pltpu.VMEM((4 * SLAB * HALF, 256), BF16),
             pltpu.VMEM((4, 8, NCOL), F32),
         ]
         + [dma] * 6
@@ -522,7 +585,7 @@
 
 
 def per_device(basis, potential, colmap, hsub_old, inv_factor, angles):
-    left = y_table_left()
+    table = y_table()
     results = main_part(
         basis.reshape(2048, 128),
         colmap.reshape(1, NCOL),
@@ -531,8 +594,8 @@
         inv_factor,
         hsub_old.T,
         jnp.asarray(x_table()),
-        jnp.asarray(left.astype(BF16)),
-        jnp.asarray(left.T.astype(BF16)),
+        jnp.asarray(table.astype(BF16)),
+        jnp.asarray(table.T.astype(BF16)),
         potential,
     )
     hblock, rotated, bands = result_part(*results)

time: 45.1 us -> 44.4 us (0.984)
  Pallas kernels: 44.3 us -> 43.6 us
    pallas_call x1, Pallas kernels: 42.5 us -> 41.8 us  [main_part(): pl.pallas_call(main_kernel, out_shape=(jax.ShapeDtypeStruct((32, 128), BF...]
where the time goes in v3:
time: 44.4 us; the launch traced here: 44.3 us
  Pallas kernels  43.6 us (98%)
  between operations  0.64 us (1%)
    pallas_call x1, Pallas kernels, main_part(): pl.pallas_call(main_kernel, out_shape=(jax.ShapeDtypeStruct((32, 128), BF...  41.8 us
    pallas_call x1, Pallas kernels, result_part(): pl.pallas_call(result_kernel, out_shape=tuple((jax.ShapeDtypeStruct(x.sha...  1.88 us

profile of v3, /device:TPU:1, one launch (start us, length us, event | category | flops | bytes accessed | tf_op | source)
XLA Modules:
  0.0 44.3 jit_solution(1430963180587678707)
XLA Ops:
  0.6 41.8 %main_part.1 = (bf16[32,128]{1,0:T(8,128)(2,1)}, f32[4,512]{1,0:T(4,128)}, bf16[32,128]{1,0:T(8,128)(2,1)}) custom-call(bf16[2048,128]{1,0:T(8,128)(2,1)} %bitcast.6, s32[1,512]{1,0:T(1,128)} %bitcast.9, f32[240,32]{1,0:T(8,128)} %bitcast.8, bf16[256,256]{1,0:T(8,128)(2,1)} %constant.8.clone.tz_in, f32[512,512]{1,0:T(8,128)} %inv_in.1, f32[504,128]{1,0:T(8,128)} %bitcast.7, ...), custom_call_target="tpu_custom_call" | custom-call | tf_op jit(solution)/shard_map/main_part/pallas_call | solution.py:510
  42.4 1.9 %result_part.1 = (bf16[32,128]{1,0:T(8,128)(2,1)}, f32[4,512]{1,0:T(4,128)}, bf16[32,128]{1,0:T(8,128)(2,1)}) custom-call(bf16[32,128]{1,0:T(8,128)(2,1)} %get-tuple-element.9.refs_0_, f32[4,512]{1,0:T(4,128)} %get-tuple-element.10.refs_1_, bf16[32,128]{1,0:T(8,128)(2,1)} %get-tuple-element.11.refs_2_), custom_call_target="tpu_custom_call" | custom-call | tf_op jit(solution)/shard_map/result_part/pallas_call | solution.py:576

commit v4 on v3

--- a/solution.py
+++ b/solution.py
@@ -230,7 +230,7 @@
     basis, columns, angles, tz, inv, hsub, tx, ty, ty_t, potential,
     state, table, low, y_buf, y_own, z_buf, rows, w_buf, bands_part,
     send1, recv1, send2, recv2, send3, recv3, sendh, gath, recvb, sendf, recvf,
-    a_cos, a_sin, phase, folded, right1, right2, radius, coef, d_buf, p_buf, g_buf,
+    q_buf, u_buf, a_cos, a_sin, phase, folded, right1, right2, radius, coef, d_buf, p_buf, g_buf,
     s1, r1, s2, r2, s3, r3, sh, rh, sb, rb, sf, rf, loads,
 ):
     band = lax.axis_index("band")
@@ -334,7 +334,6 @@
 
     copies[2].wait()
     angle_tables(angles, table)
-    rotate_back(me, state, table)
 
     for i in range(3, 7):
         copies[i].wait()
@@ -367,7 +366,6 @@
     for i in range(7, 10):
         copies[i].wait()
     fold_potential(potential, folded)
-    couple(band, state, inv, hsub, low, y_buf, y_own, z_buf)
     fft_wait_recv(*first)
 
     lanes = lax.broadcasted_iota(jnp.int32, (8, 128), 1)
@@ -382,41 +380,62 @@
                 total = jnp.where((lanes >> 4) == t, piece, total)
             coef[q, :, 128 * j : 128 * j + 128] = total
 
-    def vector(v, carry):
+    def mix(v):
         old_re, old_im = coef[2 * v], coef[2 * v + 1]
-        all_re = old_re * phase[0] - old_im * phase[1]
-        all_im = old_re * phase[1] + old_im * phase[0]
-        for z in range(SLAB):
-            for a, part in enumerate((a_cos, a_sin)):
-                for i, c in enumerate((all_re, all_im)):
-                    row = HALF * (4 * z + 2 * a + i)
-                    d_buf[row : row + HALF, :] = (part[...] * c[z : z + 1]).astype(BF16)
-        field = dot(d_buf[...], right1[...])
-        for z in range(SLAB):
-            q = []
-            for a in range(2):
-                rows_a = [field[HALF * (4 * z + 2 * a + i) :][:HALF] for i in range(2)]
-                q.append([tuple(x[:, 128 * b : 128 * b + 128] for x in rows_a) for b in range(2)])
-            back = times_potential(q, [[folded[z, u, w] for w in range(2)] for u in range(2)])
-            for a in range(2):
-                for b in range(2):
-                    for i in range(2):
-                        row = HALF * (4 * z + 2 * a + i)
-                        p_buf[row : row + HALF, 128 * b : 128 * b + 128] = back[a][b][i].astype(BF16)
-        final = dot(p_buf[...], right2[...])
-        for z in range(SLAB):
-            for i in range(2):
-                even = final[HALF * (4 * z + i) :][:HALF]
-                odd = final[HALF * (4 * z + 2 + i) :][:HALF]
-                g_buf[2 * v + i, z : z + 1, :] = jnp.sum(
-                    a_cos[...] * even + a_sin[...] * odd, axis=0, keepdims=True
-                )
+        coef[2 * v] = old_re * phase[0] - old_im * phase[1]
+        coef[2 * v + 1] = old_re * phase[1] + old_im * phase[0]
+
+    def unmix(v):
         new_re, new_im = g_buf[2 * v], g_buf[2 * v + 1]
         g_buf[2 * v] = new_re * phase[0] + new_im * phase[1]
         g_buf[2 * v + 1] = new_im * phase[0] - new_re * phase[1]
-        return carry
-
-    lax.fori_loop(0, 2, vector, 0)
+
+    def block(z, a, i):
+        return pl.ds(HALF * (4 * z + 2 * a + i), HALF)
+
+    def plane(z):
+        return pl.ds(4 * HALF * z, 4 * HALF)
+
+    def spread(v, z):
+        for a, part in enumerate((a_cos, a_sin)):
+            for i in range(2):
+                d_buf[block(z, a, i), :] = (part[...] * coef[2 * v + i, z : z + 1, :]).astype(BF16)
+
+    def to_field(v, z):
+        q_buf[plane(z), :] = dot(d_buf[plane(z), :], right1[...])
+
+    def multiply(v, z):
+        q = [
+            [tuple(q_buf[block(z, a, i), 128 * b : 128 * b + 128] for i in range(2)) for b in range(2)]
+            for a in range(2)
+        ]
+        back = times_potential(q, [[folded[z, u, w] for w in range(2)] for u in range(2)])
+        for a in range(2):
+            for b in range(2):
+                for i in range(2):
+                    p_buf[block(z, a, i), 128 * b : 128 * b + 128] = back[a][b][i].astype(BF16)
+
+    def from_field(v, z):
+        u_buf[plane(z), :] = dot(p_buf[plane(z), :], right2[...])
+
+    def collect(v, z):
+        for i in range(2):
+            g_buf[2 * v + i, z : z + 1, :] = jnp.sum(
+                a_cos[...] * u_buf[block(z, 0, i), :] + a_sin[...] * u_buf[block(z, 1, i), :],
+                axis=0,
+                keepdims=True,
+            )
+
+    steps = (spread, to_field, multiply, from_field, collect)
+
+    for v in range(2):
+        mix(v)
+    for t in range(2 * SLAB + len(steps) - 1):
+        for s, step in enumerate(steps):
+            if 0 <= t - s < 2 * SLAB:
+                step((t - s) // SLAB, (t - s) % SLAB)
+    for v in range(2):
+        unmix(v)
 
     volume = 1.0 / float(NG) ** 3
     for p in range(NFFT):
@@ -432,12 +451,8 @@
     fft_start(*second)
     recv2[pl.ds(me, 1)] = send2[pl.ds(me, 1)]
 
-    vector_weights(basis, y_own, w_buf, bands_part)
-    bands_args = (lambda to: bands_part.at[to], recvb, sb, rb)
-    for i in range(1, NBAND):
-        band_copy(i, *bands_args).start()
-    recvb[pl.ds(band, 1)] = bands_part[pl.ds(band, 1)]
-    rotate_on(state, table, rows)
+    rotate_back(me, state, table)
+    couple(band, state, inv, hsub, low, y_buf, y_own, z_buf)
 
     fft_wait_recv(*second)
     slabs = recv2[...].reshape(NFFT * 8, 128).T.astype(BF16)
@@ -456,12 +471,11 @@
     gath[pl.ds(band, 1)] = sendh[...].reshape(1, 32, 128)
     hblock_out[...] = sendh[...]
 
-    for i in range(1, NBAND):
-        band_arrival(i, *bands_args).wait_recv()
-    bands_total = recvb[0].astype(F32)
-    for b in range(1, NBAND):
-        bands_total = bands_total + recvb[b].astype(F32)
-    bands_out[...] = bands_total.astype(BF16)
+    vector_weights(basis, y_own, w_buf, bands_part)
+    bands_args = (lambda to: bands_part.at[to], recvb, sb, rb)
+    for i in range(1, NBAND):
+        band_copy(i, *bands_args).start()
+    recvb[pl.ds(band, 1)] = bands_part[pl.ds(band, 1)]
 
     for i in range(1, NBAND):
         band_arrival(i, *gather_args).wait_recv()
@@ -477,6 +491,13 @@
     third = (send3, recv3, s3, r3, True)
     fft_start(*third)
     recv3[pl.ds(me, 1)] = send3[...].reshape(1, 8, 128)
+    rotate_on(state, table, rows)
+    for i in range(1, NBAND):
+        band_arrival(i, *bands_args).wait_recv()
+    bands_total = recvb[0].astype(F32)
+    for b in range(1, NBAND):
+        bands_total = bands_total + recvb[b].astype(F32)
+    bands_out[...] = bands_total.astype(BF16)
     fft_wait_recv(*third)
     new_columns = recv3[0]
     for p in range(1, NFFT):
@@ -538,6 +559,8 @@
             pltpu.VMEM((NBAND, 32, 128), BF16),
             pltpu.VMEM((NBAND, 8, ORDER), F32),
             pltpu.VMEM((NBAND, 8, ORDER), F32),
+            pltpu.VMEM((4 * SLAB * HALF, 256), F32),
+            pltpu.VMEM((4 * SLAB * HALF, NCOL), F32),
             pltpu.VMEM((HALF, NCOL), F32),
             pltpu.VMEM((HALF, NCOL), F32),
             pltpu.VMEM((2, 8, NCOL), F32),

time: 44.4 us -> 40.6 us (0.914)
  Pallas kernels: 43.6 us -> 39.8 us
    pallas_call x1, Pallas kernels: 41.8 us -> 38 us  [main_part(): pl.pallas_call(main_kernel, out_shape=(jax.ShapeDtypeStruct((32, 128), BF...]
where the time goes in v4:
time: 40.6 us; the launch traced here: 40.5 us
  Pallas kernels  39.8 us (98%)
  between operations  0.64 us (2%)
    pallas_call x1, Pallas kernels, main_part(): pl.pallas_call(main_kernel, out_shape=(jax.ShapeDtypeStruct((32, 128), BF...  38 us
    pallas_call x1, Pallas kernels, result_part(): pl.pallas_call(result_kernel, out_shape=tuple((jax.ShapeDtypeStruct(x.sha...  1.88 us

profile of v4, /device:TPU:1, one launch (start us, length us, event | category | flops | bytes accessed | tf_op | source)
XLA Modules:
  0.0 40.5 jit_solution(18269582528341434290)
XLA Ops:
  0.6 38.0 %main_part.1 = (bf16[32,128]{1,0:T(8,128)(2,1)}, f32[4,512]{1,0:T(4,128)}, bf16[32,128]{1,0:T(8,128)(2,1)}) custom-call(bf16[2048,128]{1,0:T(8,128)(2,1)} %bitcast.6, s32[1,512]{1,0:T(1,128)} %bitcast.9, f32[240,32]{1,0:T(8,128)} %bitcast.8, bf16[256,256]{1,0:T(8,128)(2,1)} %constant.8.clone.tz_in, f32[512,512]{1,0:T(8,128)} %inv_in.1, f32[504,128]{1,0:T(8,128)} %bitcast.7, ...), custom_call_target="tpu_custom_call" | custom-call | tf_op jit(solution)/shard_map/main_part/pallas_call | solution.py:531
  38.6 1.9 %result_part.1 = (bf16[32,128]{1,0:T(8,128)(2,1)}, f32[4,512]{1,0:T(4,128)}, bf16[32,128]{1,0:T(8,128)(2,1)}) custom-call(bf16[32,128]{1,0:T(8,128)(2,1)} %get-tuple-element.9.refs_0_, f32[4,512]{1,0:T(4,128)} %get-tuple-element.10.refs_1_, bf16[32,128]{1,0:T(8,128)(2,1)} %get-tuple-element.11.refs_2_), custom_call_target="tpu_custom_call" | custom-call | tf_op jit(solution)/shard_map/result_part/pallas_call | solution.py:599

commit v5 on v4

--- a/solution.py
+++ b/solution.py
@@ -46,6 +46,11 @@
     table[:, :SLAB, 2] = np.sin(angle)
     table[:, :SLAB, 3] = np.cos(angle)
     return table.reshape(NFFT * 8, 4 * NZC)
+
+
+def z_table_back():
+    table = z_table().reshape(NFFT, 4, 2, 4 * NZC)
+    return np.transpose(table, (1, 0, 2, 3)).reshape(4 * NFFT, 8 * NZC)
 
 
 def half_angles():
@@ -225,12 +230,12 @@
 
 
 def main_kernel(
-    basis_in, columns_in, angles_in, tz_in, inv_in, hsub_in, tx_in, ty_in, ty_t_in, potential_in,
+    basis_in, columns_in, angles_in, tz_in, inv_in, hsub_in, tx_in, ty_in, ty_t_in, potential_in, tb_in,
     hblock_out, rotated_out, bands_out,
-    basis, columns, angles, tz, inv, hsub, tx, ty, ty_t, potential,
+    basis, columns, angles, tz, inv, hsub, tx, ty, ty_t, potential, tb,
     state, table, low, y_buf, y_own, z_buf, rows, w_buf, bands_part,
-    send1, recv1, send2, recv2, send3, recv3, sendh, gath, recvb, sendf, recvf,
-    q_buf, u_buf, a_cos, a_sin, phase, folded, right1, right2, radius, coef, d_buf, p_buf, g_buf,
+    send1, recv1, send2, recv2, send3, recv3, new_own, news, hall, recvb, sendf, recvf,
+    q_buf, u_buf, a_cos, a_sin, phase, phase_out, folded, right1, right2, radius, coef, d_buf, p_buf, g_buf,
     s1, r1, s2, r2, s3, r3, sh, rh, sb, rb, sf, rf, loads,
 ):
     band = lax.axis_index("band")
@@ -238,7 +243,7 @@
 
     inputs = (
         (basis_in, basis), (tz_in, tz), (angles_in, angles), (columns_in, columns), (tx_in, tx),
-        (ty_in, ty), (ty_t_in, ty_t), (inv_in, inv), (hsub_in, hsub), (potential_in, potential),
+        (ty_in, ty), (ty_t_in, ty_t), (inv_in, inv), (potential_in, potential), (tb_in, tb), (hsub_in, hsub),
     )
     copies = [pltpu.make_async_copy(a, b, loads.at[i]) for i, (a, b) in enumerate(inputs)]
     for copy in copies:
@@ -334,6 +339,12 @@
 
     copies[2].wait()
     angle_tables(angles, table)
+
+    new_args = (lambda to: new_own, news, sh, rh)
+    new_own[...] = basis[2016:2048, :]
+    for i in range(1, NBAND):
+        band_copy(i, *new_args).start()
+    news[pl.ds(band, 1)] = new_own[...].reshape(1, 32, 128)
 
     for i in range(3, 7):
         copies[i].wait()
@@ -358,12 +369,14 @@
     center = jnp.broadcast_to(turns * (math.pi / NG), (8, NCOL))
     phase[0] = jnp.cos(center)
     phase[1] = jnp.sin(center)
+    for j in range(4):
+        phase_out[:, 4 * j : 4 * j + 4, :] = phase[:, 0:4, 128 * j : 128 * j + 128]
     freq_x = jnp.where(pos_x < NG // 2, pos_x, pos_x - NG)
     freq_y = jnp.where(pos_y < NG // 2, pos_y, pos_y - NG)
     radius[...] = jnp.broadcast_to(freq_x * freq_x + freq_y * freq_y, (128, NCOL)).T
     g_buf[...] = jnp.zeros_like(g_buf)
 
-    for i in range(7, 10):
+    for i in range(7, 11):
         copies[i].wait()
     fold_potential(potential, folded)
     fft_wait_recv(*first)
@@ -386,9 +399,10 @@
         coef[2 * v + 1] = old_re * phase[1] + old_im * phase[0]
 
     def unmix(v):
-        new_re, new_im = g_buf[2 * v], g_buf[2 * v + 1]
-        g_buf[2 * v] = new_re * phase[0] + new_im * phase[1]
-        g_buf[2 * v + 1] = new_im * phase[0] - new_re * phase[1]
+        for q in (2 * v, 2 * v + 4):
+            new_re, new_im = g_buf[q], g_buf[q + 1]
+            g_buf[q] = new_re * phase_out[0] + new_im * phase_out[1]
+            g_buf[q + 1] = new_im * phase_out[0] - new_re * phase_out[1]
 
     def block(z, a, i):
         return pl.ds(HALF * (4 * z + 2 * a + i), HALF)
@@ -420,11 +434,15 @@
 
     def collect(v, z):
         for i in range(2):
-            g_buf[2 * v + i, z : z + 1, :] = jnp.sum(
+            total = jnp.sum(
                 a_cos[...] * u_buf[block(z, 0, i), :] + a_sin[...] * u_buf[block(z, 1, i), :],
                 axis=0,
                 keepdims=True,
             )
+            for j in range(4):
+                g_buf[4 * (z % 2) + 2 * v + i, 4 * j + z // 2 : 4 * j + z // 2 + 1, :] = total[
+                    :, 128 * j : 128 * j + 128
+                ]
 
     steps = (spread, to_field, multiply, from_field, collect)
 
@@ -438,49 +456,76 @@
         unmix(v)
 
     volume = 1.0 / float(NG) ** 3
-    for p in range(NFFT):
-        total = jnp.zeros((8, 128), F32)
-        for q in range(4):
-            piece = g_buf[q, :, 128 * (p // 8) : 128 * (p // 8) + 128]
-            move = (16 * q - 16 * (p % 8)) % 128
+    wide_lanes = lax.broadcasted_iota(jnp.int32, (16, 128), 1)
+    for t in range(8):
+        total = jnp.zeros((16, 128), F32)
+        for q in range(8):
+            piece = g_buf[q]
+            move = (16 * q - 16 * t) % 128
             if move:
                 piece = pltpu.roll(piece, move, 1)
-            total = jnp.where((lanes >> 4) == q, piece, total)
-        send2[p] = total * volume
-    second = (send2, recv2, s2, r2, False)
-    fft_start(*second)
-    recv2[pl.ds(me, 1)] = send2[pl.ds(me, 1)]
-
+            total = jnp.where((wide_lanes >> 4) == q, piece, total)
+        total = total * volume
+        for j in range(4):
+            send2[8 * j + t] = total[4 * j : 4 * j + 4]
+    own = band * NFFT + me
+
+    def spread_back(i, carry):
+        to = lax.rem(own + i, NBAND * NFFT)
+        pltpu.make_async_remote_copy(
+            src_ref=send2.at[lax.rem(to, NFFT)],
+            dst_ref=recv2.at[own],
+            send_sem=s2,
+            recv_sem=r2,
+            device_id=(to // NFFT, lax.rem(to, NFFT)),
+            device_id_type=MESH,
+        ).start()
+        return carry
+
+    lax.fori_loop(1, NBAND * NFFT, spread_back, 0)
+    back_part = recv2.at[pl.ds(0, NBAND * NFFT - 1)]
+    back_all = pltpu.make_async_remote_copy(
+        src_ref=back_part,
+        dst_ref=back_part,
+        send_sem=s2,
+        recv_sem=r2,
+        device_id=(band, lax.rem(me + 1, NFFT)),
+        device_id_type=MESH,
+    )
+    recv2[pl.ds(own, 1)] = send2[pl.ds(me, 1)]
     rotate_back(me, state, table)
     couple(band, state, inv, hsub, low, y_buf, y_own, z_buf)
 
-    fft_wait_recv(*second)
-    slabs = recv2[...].reshape(NFFT * 8, 128).T.astype(BF16)
-    local = dot(slabs, tz[...])
+    vector_weights(basis, y_own, w_buf, bands_part)
+    bands_args = (lambda to: bands_part.at[to], recvb, sb, rb)
+    for i in range(1, NBAND):
+        band_copy(i, *bands_args).start()
+    recvb[pl.ds(band, 1)] = bands_part[pl.ds(band, 1)]
+    for i in range(1, NBAND):
+        band_arrival(i, *new_args).wait_recv()
     slot = lax.broadcasted_iota(jnp.int32, (16, 128), 1) & (NZC - 1)
     freq_z = jnp.where(slot < NZC // 2, slot, slot - NZC).astype(F32)
     own_radius = radius[pl.ds(pl.multiple_of(me * 16, 16), 16), :]
     kinetic = (own_radius + freq_z * freq_z) / (2.0 * (NG // 4) ** 2)
-    for v in range(2):
-        term = local[32 * v : 32 * v + 16, :128] + local[32 * v + 16 : 32 * v + 32, 128:]
-        coeffs = basis[2016 + 16 * v : 2032 + 16 * v, :].astype(F32)
-        sendh[16 * v : 16 * v + 16, :] = (kinetic * coeffs + term).astype(BF16)
-    gather_args = (lambda to: sendh, gath, sh, rh)
-    for i in range(1, NBAND):
-        band_copy(i, *gather_args).start()
-    gath[pl.ds(band, 1)] = sendh[...].reshape(1, 32, 128)
-    hblock_out[...] = sendh[...]
-
-    vector_weights(basis, y_own, w_buf, bands_part)
-    bands_args = (lambda to: bands_part.at[to], recvb, sb, rb)
-    for i in range(1, NBAND):
-        band_copy(i, *bands_args).start()
-    recvb[pl.ds(band, 1)] = bands_part[pl.ds(band, 1)]
-
-    for i in range(1, NBAND):
-        band_arrival(i, *gather_args).wait_recv()
-
-    pairs = dot_nt(basis[...], gath[...].reshape(128, 128))
+
+    back_all.wait_recv()
+    slabs = []
+    for b in range(NBAND):
+        parts = [recv2[NFFT * b : NFFT * b + NFFT, r, :] for r in range(3)]
+        parts.append(jnp.zeros((NFFT, 128), F32))
+        slabs.append(jnp.concatenate(parts, 0).T.astype(BF16))
+    local = dot(jnp.concatenate(slabs, 0), tb[...])
+    for b in range(NBAND):
+        for v in range(2):
+            term = jnp.zeros((16, 128), F32)
+            for n in range(2):
+                row, lane = 128 * b + 64 * n + 32 * v, 256 * n
+                term = term + local[row : row + 16, lane : lane + 128]
+                term = term + local[row + 16 : row + 32, lane + 128 : lane + 256]
+            coeffs = news[b, 16 * v : 16 * v + 16, :].astype(F32)
+            hall[b, 16 * v : 16 * v + 16, :] = (kinetic * coeffs + term).astype(BF16)
+
+    pairs = dot_nt(basis[...], hall[...].reshape(128, 128))
     pair_row = lax.broadcasted_iota(jnp.int32, (2048, 128), 0)
     pair_lane = lax.broadcasted_iota(jnp.int32, (2048, 128), 1)
     pairs = jnp.where(((pair_row ^ pair_lane) & 15) == 0, pairs, 0.0)
@@ -492,6 +537,7 @@
     fft_start(*third)
     recv3[pl.ds(me, 1)] = send3[...].reshape(1, 8, 128)
     rotate_on(state, table, rows)
+    hblock_out[...] = hall[pl.ds(band, 1)].reshape(32, 128)
     for i in range(1, NBAND):
         band_arrival(i, *bands_args).wait_recv()
     bands_total = recvb[0].astype(F32)
@@ -512,11 +558,11 @@
     recvf[pl.ds(band, 1)] = sendf[pl.ds(band, 1)]
 
     fft_wait_send(*first)
-    fft_wait_send(*second)
+    back_all.wait_send()
     fft_wait_send(*third)
     for i in range(1, NBAND):
         band_copy(i, *bands_args).wait_send()
-        band_copy(i, *gather_args).wait_send()
+        band_copy(i, *new_args).wait_send()
     for i in range(1, NBAND):
         band_arrival(i, *final_args).wait_recv()
     final = recvf[0] + recvf[1] + recvf[2] + recvf[3]
@@ -550,11 +596,12 @@
             pltpu.VMEM((NBAND, 32, 128), BF16),
             pltpu.VMEM((NFFT, 8, 128), F32),
             pltpu.VMEM((NFFT, 8, 128), F32),
-            pltpu.VMEM((NFFT, 8, 128), F32),
-            pltpu.VMEM((NFFT, 8, 128), F32),
+            pltpu.VMEM((NFFT, 4, 128), F32),
+            pltpu.VMEM((NBAND * NFFT, 4, 128), F32),
             pltpu.VMEM((8, 128), F32),
             pltpu.VMEM((NFFT, 8, 128), F32),
             pltpu.VMEM((32, 128), BF16),
+            pltpu.VMEM((NBAND, 32, 128), BF16),
             pltpu.VMEM((NBAND, 32, 128), BF16),
             pltpu.VMEM((NBAND, 32, 128), BF16),
             pltpu.VMEM((NBAND, 8, ORDER), F32),
@@ -564,6 +611,7 @@
             pltpu.VMEM((HALF, NCOL), F32),
             pltpu.VMEM((HALF, NCOL), F32),
             pltpu.VMEM((2, 8, NCOL), F32),
+            pltpu.VMEM((2, 16, 128), F32),
             pltpu.VMEM((SLAB, 2, 2, HALF, 128), F32),
             pltpu.VMEM((NCOL, 256), BF16),
             pltpu.VMEM((256, NCOL), BF16),
@@ -571,7 +619,7 @@
             pltpu.VMEM((4, 8, NCOL), F32),
             pltpu.VMEM((4 * SLAB * HALF, NCOL), BF16),
             pltpu.VMEM((4 * SLAB * HALF, 256), BF16),
-            pltpu.VMEM((4, 8, NCOL), F32),
+            pltpu.VMEM((8, 16, 128), F32),
         ]
         + [dma] * 6
         + [dma((NBAND,))] * 6
@@ -620,6 +668,7 @@
         jnp.asarray(table.astype(BF16)),
         jnp.asarray(table.T.astype(BF16)),
         potential,
+        jnp.asarray(z_table_back().astype(BF16)),
     )
     hblock, rotated, bands = result_part(*results)
     return (hblock.reshape(2, 16, 128), rotated, bands.reshape(2, 16, 128))

time: 40.6 us -> 39.4 us (0.970)
  Pallas kernels: 39.8 us -> 38.7 us
    pallas_call x1, Pallas kernels: 38 us -> 36.8 us  [main_part(): pl.pallas_call(main_kernel, out_shape=(jax.ShapeDtypeStruct((32, 128), BF...]
where the time goes in v5:
time: 39.4 us; the launch traced here: 39.3 us
  Pallas kernels  38.7 us (98%)
  between operations  0.64 us (2%)
    pallas_call x1, Pallas kernels, main_part(): pl.pallas_call(main_kernel, out_shape=(jax.ShapeDtypeStruct((32, 128), BF...  36.8 us
    pallas_call x1, Pallas kernels, result_part(): pl.pallas_call(result_kernel, out_shape=tuple((jax.ShapeDtypeStruct(x.sha...  1.88 us

profile of v5, /device:TPU:1, one launch (start us, length us, event | category | flops | bytes accessed | tf_op | source)
XLA Modules:
  0.0 39.3 jit_solution(9517866832642281215)
XLA Ops:
  0.6 36.8 %main_part.1 = (bf16[32,128]{1,0:T(8,128)(2,1)}, f32[4,512]{1,0:T(4,128)}, bf16[32,128]{1,0:T(8,128)(2,1)}) custom-call(bf16[2048,128]{1,0:T(8,128)(2,1)} %bitcast.6, s32[1,512]{1,0:T(1,128)} %bitcast.9, f32[240,32]{1,0:T(8,128)} %bitcast.8, bf16[256,256]{1,0:T(8,128)(2,1)} %constant.10.clone.tz_in, f32[512,512]{1,0:T(8,128)} %inv_in.1, f32[504,128]{1,0:T(8,128)} %bitcast.7, ...), custom_call_target="tpu_custom_call" | custom-call | tf_op jit(solution)/shard_map/main_part/pallas_call | solution.py:577
  37.4 1.9 %result_part.1 = (bf16[32,128]{1,0:T(8,128)(2,1)}, f32[4,512]{1,0:T(4,128)}, bf16[32,128]{1,0:T(8,128)(2,1)}) custom-call(bf16[32,128]{1,0:T(8,128)(2,1)} %get-tuple-element.9.refs_0_, f32[4,512]{1,0:T(4,128)} %get-tuple-element.10.refs_1_, bf16[32,128]{1,0:T(8,128)(2,1)} %get-tuple-element.11.refs_2_), custom_call_target="tpu_custom_call" | custom-call | tf_op jit(solution)/shard_map/result_part/pallas_call | solution.py:647

commit v6 on v5

--- a/solution.py
+++ b/solution.py
@@ -81,7 +81,7 @@
     return seat[:8] + seat[:7:-1]
 
 
-def pair_step(state, table, r, forward):
+def pair_step(state, table, r):
     src, dst = state.at[r % 2], state.at[(r + 1) % 2]
     shift = r % TILE
     c = table[0, 8 * r : 8 * r + 8]
@@ -90,27 +90,14 @@
     b = src[8:16]
     if shift:
         b = pltpu.roll(b, TILE - shift, 1)
-    if forward:
-        a, b = c * a - s * b, s * a + c * b
-    else:
-        a, b = c * a + s * b, c * b - s * a
+    a, b = c * a - s * b, s * a + c * b
     if shift:
         b = pltpu.roll(b, shift, 1)
-    if forward:
-        dst[0:1] = a[0:1]
-        dst[1:7] = a[2:8]
-        dst[7:8] = b[7:8]
-        dst[8:9] = a[1:2]
-        dst[9:16] = b[0:7]
-    elif r:
-        dst[0:1] = a[0:1]
-        dst[2:8] = a[1:7]
-        dst[15:16] = a[7:8]
-        dst[1:2] = b[0:1]
-        dst[8:15] = b[1:8]
-    else:
-        dst[0:8] = a
-        dst[8:16] = b
+    dst[0:1] = a[0:1]
+    dst[1:7] = a[2:8]
+    dst[7:8] = b[7:8]
+    dst[8:9] = a[1:2]
+    dst[9:16] = b[0:7]
 
 
 def angle_tables(angles, table):
@@ -121,30 +108,31 @@
             table[i, q] = jnp.broadcast_to(part[:, q : q + 1], (TILE, 128))
 
 
-def rotate_back(me, state, table):
-    row = lax.broadcasted_iota(jnp.int32, (TILE, 128), 0)
-    lane = lax.broadcasted_iota(jnp.int32, (TILE, 128), 1)
-    target = ((lane >> 3) * NFFT + me) * 4 + (lane & 7)
-    target = jnp.where((lane < 32) & ((lane & 7) < 4), target, -1)
-    target = jnp.where((lane >= 32) & (lane < 40), lane - 32, target)
-    for p, tile in enumerate(tile_order(14)):
-        state[1, p] = (row + TILE * tile == target).astype(F32)
-    for r in range(ROUNDS - 1, -1, -1):
-        pair_step(state, table, r, False)
+def rotate_factor(band, state, table, inv, factor):
+    own = inv[:, pl.ds(pl.multiple_of(band * GROUP, GROUP), GROUP)]
+    for p, tile in enumerate(tile_order(0)):
+        state[0, p] = own[TILE * tile : TILE * tile + TILE]
+    for r in range(ROUNDS):
+        pair_step(state, table, r)
+    factor[...] = natural(state, 0)
 
 
 def natural(state, which):
     return jnp.concatenate([state[which, p] for p in list(range(8)) + list(range(15, 7, -1))], 0)
 
 
-def couple(band, state, inv, hsub, low, y_buf, y_own, z_buf):
+def couple(me, state, inv, hsub, low, factor, factor_wide, y_own, z_buf):
     low[...] = inv[...].astype(BF16)
-    y_buf[...] = dot(natural(state, 1).T.astype(BF16), low[...])
-    own = y_buf[:, pl.ds(pl.multiple_of(band * GROUP, GROUP), GROUP)]
+    for j in range(4):
+        factor_wide[:, GROUP * j : GROUP * j + GROUP] = factor[pl.ds(j, 128, stride=4), :].astype(BF16)
+    line = lax.broadcasted_iota(jnp.int32, (128, ORDER), 0)
+    column = lax.broadcasted_iota(jnp.int32, (128, ORDER), 1)
+    target = ((line >> 3) * NFFT + me) * 4 + (line & 7)
+    target = jnp.where((line < 32) & ((line & 7) < 4), target, -1)
+    target = jnp.where((line >= 32) & (line < 40), line - 32, target)
+    own = dot((column == target).astype(F32).astype(BF16), factor[...].astype(BF16))
     y_own[...] = own[:40]
     z_old = dot_nt(hsub[...].astype(BF16), own.astype(BF16))
-    lane = lax.broadcasted_iota(jnp.int32, (8, 128), 1)
-    row = lax.broadcasted_iota(jnp.int32, (8, 128), 0)
     z_buf[...] = jnp.zeros_like(z_buf)
     for b in range(NBAND):
         z_buf[b * GROUP : b * GROUP + 126, :] = z_old[b * 126 : (b + 1) * 126, :]
@@ -160,7 +148,7 @@
 
 def rotate_on(state, table, rows):
     for r in range(ROUNDS):
-        pair_step(state, table, r, True)
+        pair_step(state, table, r)
     rows[...] = natural(state, 0).T[:40]
 
 
@@ -229,11 +217,29 @@
     return (add(s1, s2), (odd_y[1], -odd_y[0])), ((odd_x[1], -odd_x[0]), sub(s2, s1))
 
 
+def hops(steps):
+    z_hi, core, z_lo, x, y = steps
+    return (1 if z_lo else 2 * z_hi) + min(x, 4 - x) + min(y, 4 - y)
+
+
+def all_steps(bands):
+    found = [
+        (z_hi, core, z_lo, x, y)
+        for z_hi in range(bands)
+        for core in range(bands)
+        for z_lo in range(2)
+        for x in range(4)
+        for y in range(4)
+    ]
+    found.remove((0, 0, 0, 0, 0))
+    return sorted(found, key=lambda s: -hops(s))
+
+
 def main_kernel(
     basis_in, columns_in, angles_in, tz_in, inv_in, hsub_in, tx_in, ty_in, ty_t_in, potential_in, tb_in,
     hblock_out, rotated_out, bands_out,
     basis, columns, angles, tz, inv, hsub, tx, ty, ty_t, potential, tb,
-    state, table, low, y_buf, y_own, z_buf, rows, w_buf, bands_part,
+    state, table, low, factor, factor_wide, y_own, z_buf, rows, w_buf, bands_part,
     send1, recv1, send2, recv2, send3, recv3, new_own, news, hall, recvb, sendf, recvf,
     q_buf, u_buf, a_cos, a_sin, phase, phase_out, folded, right1, right2, radius, coef, d_buf, p_buf, g_buf,
     s1, r1, s2, r2, s3, r3, sh, rh, sb, rb, sf, rf, loads,
@@ -246,37 +252,39 @@
         (ty_in, ty), (ty_t_in, ty_t), (inv_in, inv), (potential_in, potential), (tb_in, tb), (hsub_in, hsub),
     )
     copies = [pltpu.make_async_copy(a, b, loads.at[i]) for i, (a, b) in enumerate(inputs)]
-    for copy in copies:
-        copy.start()
+    copies[0].start()
+    copies[1].start()
+
+    def peer(steps):
+        z_hi, core, z_lo, x, y = steps
+        to_fft = (((me >> 4) ^ z_lo) << 4) | ((((me >> 2) + x) & 3) << 2) | ((me + y) & 3)
+        return (band ^ (2 * z_hi + core), to_fft)
+
+    near, every = all_steps(1), all_steps(2)
 
     barrier = pltpu.get_barrier_semaphore()
 
-    def greet(i, carry):
-        pl.semaphore_signal(
-            barrier, inc=1, device_id=(band, lax.rem(me + i, NFFT)), device_id_type=MESH
-        )
-        return carry
-
-    lax.fori_loop(1, NFFT, greet, 0)
+    for steps in near:
+        pl.semaphore_signal(barrier, inc=1, device_id=peer(steps), device_id_type=MESH)
     for i in range(1, NBAND):
         pl.semaphore_signal(
             barrier, inc=1, device_id=(lax.rem(band + i, NBAND), me), device_id_type=MESH
         )
 
+    for copy in copies[2:]:
+        copy.start()
+
     def fft_start(send, recv, ssem, rsem, whole):
-        def step(i, carry):
-            to = lax.rem(me + i, NFFT)
+        for steps in near:
+            to = peer(steps)
             pltpu.make_async_remote_copy(
-                src_ref=send if whole else send.at[to],
+                src_ref=send if whole else send.at[to[1]],
                 dst_ref=recv.at[me],
                 send_sem=ssem,
                 recv_sem=rsem,
-                device_id=(band, to),
+                device_id=to,
                 device_id_type=MESH,
             ).start()
-            return carry
-
-        lax.fori_loop(1, NFFT, step, 0)
 
     def fft_all(send, recv, ssem, rsem, whole):
         part = recv.at[pl.ds(0, NFFT - 1)]
@@ -470,19 +478,16 @@
             send2[8 * j + t] = total[4 * j : 4 * j + 4]
     own = band * NFFT + me
 
-    def spread_back(i, carry):
-        to = lax.rem(own + i, NBAND * NFFT)
+    for steps in every:
+        to = peer(steps)
         pltpu.make_async_remote_copy(
-            src_ref=send2.at[lax.rem(to, NFFT)],
+            src_ref=send2.at[to[1]],
             dst_ref=recv2.at[own],
             send_sem=s2,
             recv_sem=r2,
-            device_id=(to // NFFT, lax.rem(to, NFFT)),
+            device_id=to,
             device_id_type=MESH,
         ).start()
-        return carry
-
-    lax.fori_loop(1, NBAND * NFFT, spread_back, 0)
     back_part = recv2.at[pl.ds(0, NBAND * NFFT - 1)]
     back_all = pltpu.make_async_remote_copy(
         src_ref=back_part,
@@ -493,14 +498,15 @@
         device_id_type=MESH,
     )
     recv2[pl.ds(own, 1)] = send2[pl.ds(me, 1)]
-    rotate_back(me, state, table)
-    couple(band, state, inv, hsub, low, y_buf, y_own, z_buf)
-
-    vector_weights(basis, y_own, w_buf, bands_part)
-    bands_args = (lambda to: bands_part.at[to], recvb, sb, rb)
+    rotate_factor(band, state, table, inv, factor)
+    couple(me, state, inv, hsub, low, factor, factor_wide, y_own, z_buf)
+    rotate_on(state, table, rows)
+    sendf[...] = rows[0:32, :].reshape(NBAND, 8, ORDER)
+    final_args = (lambda to: sendf.at[to], recvf, sf, rf)
     for i in range(1, NBAND):
-        band_copy(i, *bands_args).start()
-    recvb[pl.ds(band, 1)] = bands_part[pl.ds(band, 1)]
+        band_copy(i, *final_args).start()
+    recvf[pl.ds(band, 1)] = sendf[pl.ds(band, 1)]
+
     for i in range(1, NBAND):
         band_arrival(i, *new_args).wait_recv()
     slot = lax.broadcasted_iota(jnp.int32, (16, 128), 1) & (NZC - 1)
@@ -530,13 +536,40 @@
     pair_lane = lax.broadcasted_iota(jnp.int32, (2048, 128), 1)
     pairs = jnp.where(((pair_row ^ pair_lane) & 15) == 0, pairs, 0.0)
     by_group = jnp.sum(pairs.reshape(GROUP, 16, 128), axis=1)
-    pick_row = lax.broadcasted_iota(jnp.int32, (8, 128), 0)
-    pick = (pick_row == (lanes >> 4)).astype(F32)
-    send3[...] = dot_nt(pick, by_group, HIGH)
-    third = (send3, recv3, s3, r3, True)
-    fft_start(*third)
-    recv3[pl.ds(me, 1)] = send3[...].reshape(1, 8, 128)
-    rotate_on(state, table, rows)
+    pick_row = lax.broadcasted_iota(jnp.int32, (128, 512), 0)
+    pick_lane = lax.broadcasted_iota(jnp.int32, (128, 512), 1)
+    slot_of = pick_lane & 127
+    picked = ((slot_of >> 3) == (pick_lane >> 7)) & ((slot_of & 7) == (pick_row >> 4))
+    pick = picked.astype(F32).astype(BF16)
+    high, low_part = split(by_group)
+    fresh = dot(high, pick) + dot(low_part, pick)
+    fresh = jnp.concatenate([fresh[:, 128 * j : 128 * j + 128] for j in range(4)], 0).astype(BF16)
+    send3[...] = dot(factor_wide[...], fresh).reshape(NBAND * NFFT, 1, 128)
+    for steps in every:
+        to = peer(steps)
+        pltpu.make_async_remote_copy(
+            src_ref=send3.at[to[0] * NFFT + to[1]],
+            dst_ref=recv3.at[own],
+            send_sem=s3,
+            recv_sem=r3,
+            device_id=to,
+            device_id_type=MESH,
+        ).start()
+    sum_part = recv3.at[pl.ds(0, NBAND * NFFT - 1)]
+    sum_all = pltpu.make_async_remote_copy(
+        src_ref=sum_part,
+        dst_ref=sum_part,
+        send_sem=s3,
+        recv_sem=r3,
+        device_id=(band, lax.rem(me + 1, NFFT)),
+        device_id_type=MESH,
+    )
+    recv3[pl.ds(own, 1)] = send3[pl.ds(own, 1)]
+    vector_weights(basis, y_own, w_buf, bands_part)
+    bands_args = (lambda to: bands_part.at[to], recvb, sb, rb)
+    for i in range(1, NBAND):
+        band_copy(i, *bands_args).start()
+    recvb[pl.ds(band, 1)] = bands_part[pl.ds(band, 1)]
     hblock_out[...] = hall[pl.ds(band, 1)].reshape(32, 128)
     for i in range(1, NBAND):
         band_arrival(i, *bands_args).wait_recv()
@@ -544,31 +577,25 @@
     for b in range(1, NBAND):
         bands_total = bands_total + recvb[b].astype(F32)
     bands_out[...] = bands_total.astype(BF16)
-    fft_wait_recv(*third)
-    new_columns = recv3[0]
-    for p in range(1, NFFT):
-        new_columns = new_columns + recv3[p]
-    new_columns = new_columns * (1.0 / math.sqrt(2 * NCOL * NZC))
-    z_new = dot_nt(y_own[0:32, :], new_columns, HIGH)
-    total = rows[0:32, :] + dot(z_new, rows[32:40, :], HIGH)
-    sendf[...] = total.reshape(NBAND, 8, ORDER)
-    final_args = (lambda to: sendf.at[to], recvf, sf, rf)
     for i in range(1, NBAND):
-        band_copy(i, *final_args).start()
-    recvf[pl.ds(band, 1)] = sendf[pl.ds(band, 1)]
-
+        band_arrival(i, *final_args).wait_recv()
+    old_part = recvf[0] + recvf[1] + recvf[2] + recvf[3]
+    wide_rows = jnp.concatenate([rows[32:40, :]] * 4 + [jnp.zeros((96, ORDER), F32)], 0).astype(BF16)
     fft_wait_send(*first)
     back_all.wait_send()
-    fft_wait_send(*third)
     for i in range(1, NBAND):
         band_copy(i, *bands_args).wait_send()
         band_copy(i, *new_args).wait_send()
-    for i in range(1, NBAND):
-        band_arrival(i, *final_args).wait_recv()
-    final = recvf[0] + recvf[1] + recvf[2] + recvf[3]
-    rotated_out[...] = final[0:4]
-    for i in range(1, NBAND):
         band_copy(i, *final_args).wait_send()
+
+    sum_all.wait_recv()
+    total = jnp.sum(recv3[...].reshape(NBAND * NFFT, 128), axis=0, keepdims=True)
+    total = total * (1.0 / math.sqrt(2 * NCOL * NZC))
+    spread_rows = lax.broadcasted_iota(jnp.int32, (8, 128), 0)
+    total = jnp.where((lanes >> 3) == spread_rows, total, 0.0)
+    new_part = dot(total.astype(BF16), wide_rows)
+    rotated_out[...] = (old_part + new_part)[0:4]
+    sum_all.wait_send()
 
 
 def main_part(*operands):
@@ -588,7 +615,8 @@
             pltpu.VMEM((2, 16, TILE, 128), F32),
             pltpu.VMEM((2, 8 * ROUNDS, TILE, 128), F32),
             pltpu.VMEM((ORDER, ORDER), BF16),
-            pltpu.VMEM((128, ORDER), F32),
+            pltpu.VMEM((ORDER, 128), F32),
+            pltpu.VMEM((128, ORDER), BF16),
             pltpu.VMEM((40, GROUP), F32),
             pltpu.VMEM((ORDER, 128), F32),
             pltpu.VMEM((40, ORDER), F32),
@@ -598,8 +626,8 @@
             pltpu.VMEM((NFFT, 8, 128), F32),
             pltpu.VMEM((NFFT, 4, 128), F32),
             pltpu.VMEM((NBAND * NFFT, 4, 128), F32),
-            pltpu.VMEM((8, 128), F32),
-            pltpu.VMEM((NFFT, 8, 128), F32),
+            pltpu.VMEM((NBAND * NFFT, 1, 128), F32),
+            pltpu.VMEM((NBAND * NFFT, 1, 128), F32),
             pltpu.VMEM((32, 128), BF16),
             pltpu.VMEM((NBAND, 32, 128), BF16),
             pltpu.VMEM((NBAND, 32, 128), BF16),

time: 39.4 us -> 34.9 us (0.89)
  Pallas kernels: 38.7 us -> 33.9 us
    pallas_call x1, Pallas kernels: 36.8 us -> 32.1 us  [main_part(): pl.pallas_call(main_kernel, out_shape=(jax.ShapeDtypeStruct((32, 128), BF...]
where the time goes in v6:
time: 34.9 us; the launch traced here: 34.7 us
  Pallas kernels  33.9 us (97%)
  between operations  0.8 us (2%)
    pallas_call x1, Pallas kernels, main_part(): pl.pallas_call(main_kernel, out_shape=(jax.ShapeDtypeStruct((32, 128), BF...  32.1 us
    pallas_call x1, Pallas kernels, result_part(): pl.pallas_call(result_kernel, out_shape=tuple((jax.ShapeDtypeStruct(x.sha...  1.88 us

profile of v6, /device:TPU:1, one launch (start us, length us, event | category | flops | bytes accessed | tf_op | source)
XLA Modules:
  0.0 34.7 jit_solution(18146549238851115701)
XLA Ops:
  0.6 32.1 %main_part.1 = (bf16[32,128]{1,0:T(8,128)(2,1)}, f32[4,512]{1,0:T(4,128)}, bf16[32,128]{1,0:T(8,128)(2,1)}) custom-call(bf16[2048,128]{1,0:T(8,128)(2,1)} %bitcast.6, s32[1,512]{1,0:T(1,128)} %bitcast.9, f32[240,32]{1,0:T(8,128)} %bitcast.8, bf16[256,256]{1,0:T(8,128)(2,1)} %constant.10.clone.tz_in, f32[512,512]{1,0:T(8,128)} %inv_in.1, f32[504,128]{1,0:T(8,128)} %bitcast.7, ...), custom_call_target="tpu_custom_call" | custom-call | tf_op jit(solution)/shard_map/main_part/pallas_call | solution.py:604
  32.7 1.9 %result_part.1 = (bf16[32,128]{1,0:T(8,128)(2,1)}, f32[4,512]{1,0:T(4,128)}, bf16[32,128]{1,0:T(8,128)(2,1)}) custom-call(bf16[32,128]{1,0:T(8,128)(2,1)} %get-tuple-element.9.refs_0_, f32[4,512]{1,0:T(4,128)} %get-tuple-element.10.refs_1_, bf16[32,128]{1,0:T(8,128)(2,1)} %get-tuple-element.11.refs_2_), custom_call_target="tpu_custom_call" | custom-call | tf_op jit(solution)/shard_map/result_part/pallas_call | solution.py:675

commit v7 on v6

--- a/solution.py
+++ b/solution.py
@@ -19,6 +19,7 @@
 NFFT = 32
 SLAB = 6
 ROUNDS = 30
+SPLIT = 15
 TILE = 32
 F32 = jnp.float32
 BF16 = jnp.bfloat16
@@ -100,12 +101,17 @@
     dst[9:16] = b[0:7]
 
 
-def angle_tables(angles, table):
+def turn_angles(angles, turned):
     ang = jnp.concatenate([angles[...], jnp.zeros((240, 128 - TILE), F32)], 1)
     ang = jnp.concatenate([ang, jnp.zeros((16, 128), F32)], 0)
-    for i, part in enumerate((jnp.cos(ang).T[:TILE], jnp.sin(ang).T[:TILE])):
-        for q in range(8 * ROUNDS):
-            table[i, q] = jnp.broadcast_to(part[:, q : q + 1], (TILE, 128))
+    turned[0] = jnp.cos(ang).T[:TILE]
+    turned[1] = jnp.sin(ang).T[:TILE]
+
+
+def angle_tables(turned, table, start, stop):
+    for i in range(2):
+        for q in range(8 * start, 8 * stop):
+            table[i, q] = jnp.broadcast_to(turned[i, :, q : q + 1], (TILE, 128))
 
 
 def rotate_factor(band, state, table, inv, factor):
@@ -121,8 +127,7 @@
     return jnp.concatenate([state[which, p] for p in list(range(8)) + list(range(15, 7, -1))], 0)
 
 
-def couple(me, state, inv, hsub, low, factor, factor_wide, y_own, z_buf):
-    low[...] = inv[...].astype(BF16)
+def couple(me, hsub, factor, factor_wide, y_own, z_buf, sendz, sendr):
     for j in range(4):
         factor_wide[:, GROUP * j : GROUP * j + GROUP] = factor[pl.ds(j, 128, stride=4), :].astype(BF16)
     line = lax.broadcasted_iota(jnp.int32, (128, ORDER), 0)
@@ -136,20 +141,10 @@
     z_buf[...] = jnp.zeros_like(z_buf)
     for b in range(NBAND):
         z_buf[b * GROUP : b * GROUP + 126, :] = z_old[b * 126 : (b + 1) * 126, :]
-    lanes = lax.broadcasted_iota(jnp.int32, (ORDER, 128), 1)
-    rows = lax.broadcasted_iota(jnp.int32, (ORDER, 128), 0)
-    fresh = ((lanes - 32) >> 1) * GROUP + 126 + (lanes & 1)
-    z = jnp.where(lanes < 32, z_buf[...], 0.0)
-    z = jnp.where((lanes >= 32) & (lanes < 40) & (rows == fresh), 1.0, z)
-    w = dot(low[...], z.astype(BF16))
-    for p, tile in enumerate(tile_order(0)):
-        state[0, p] = w[TILE * tile : TILE * tile + TILE]
-
-
-def rotate_on(state, table, rows):
-    for r in range(ROUNDS):
-        pair_step(state, table, r)
-    rows[...] = natural(state, 0).T[:40]
+    z_rows = z_buf[...].T[:32]
+    for b in range(NBAND):
+        sendz[b] = z_rows[:, GROUP * b : GROUP * b + GROUP]
+    sendr[...] = factor[...].T[120:128]
 
 
 def vector_weights(basis, y_own, w_buf, bands_part):
@@ -239,10 +234,10 @@
     basis_in, columns_in, angles_in, tz_in, inv_in, hsub_in, tx_in, ty_in, ty_t_in, potential_in, tb_in,
     hblock_out, rotated_out, bands_out,
     basis, columns, angles, tz, inv, hsub, tx, ty, ty_t, potential, tb,
-    state, table, low, factor, factor_wide, y_own, z_buf, rows, w_buf, bands_part,
+    state, turned, table, factor, factor_wide, y_own, z_buf, sendz, recvz, sendr, recvr, w_buf, bands_part,
     send1, recv1, send2, recv2, send3, recv3, new_own, news, hall, recvb, sendf, recvf,
     q_buf, u_buf, a_cos, a_sin, phase, phase_out, folded, right1, right2, radius, coef, d_buf, p_buf, g_buf,
-    s1, r1, s2, r2, s3, r3, sh, rh, sb, rb, sf, rf, loads,
+    s1, r1, s2, r2, s3, r3, sh, rh, sb, rb, sf, rf, sz, rz, sr, rr, loads,
 ):
     band = lax.axis_index("band")
     me = lax.axis_index("fft")
@@ -346,7 +341,8 @@
     recv1[pl.ds(me, 1)] = send1[pl.ds(me, 1)]
 
     copies[2].wait()
-    angle_tables(angles, table)
+    turn_angles(angles, turned)
+    angle_tables(turned, table, 0, SPLIT)
 
     new_args = (lambda to: new_own, news, sh, rh)
     new_own[...] = basis[2016:2048, :]
@@ -481,14 +477,14 @@
     for steps in every:
         to = peer(steps)
         pltpu.make_async_remote_copy(
-            src_ref=send2.at[to[1]],
-            dst_ref=recv2.at[own],
+            src_ref=send2.at[to[1], pl.ds(0, 3)],
+            dst_ref=recv2.at[own, pl.ds(0, 3)],
             send_sem=s2,
             recv_sem=r2,
             device_id=to,
             device_id_type=MESH,
         ).start()
-    back_part = recv2.at[pl.ds(0, NBAND * NFFT - 1)]
+    back_part = recv2.at[pl.ds(0, NBAND * NFFT - 1), pl.ds(0, 3)]
     back_all = pltpu.make_async_remote_copy(
         src_ref=back_part,
         dst_ref=back_part,
@@ -498,15 +494,23 @@
         device_id_type=MESH,
     )
     recv2[pl.ds(own, 1)] = send2[pl.ds(me, 1)]
+    angle_tables(turned, table, SPLIT, ROUNDS)
     rotate_factor(band, state, table, inv, factor)
-    couple(me, state, inv, hsub, low, factor, factor_wide, y_own, z_buf)
-    rotate_on(state, table, rows)
-    sendf[...] = rows[0:32, :].reshape(NBAND, 8, ORDER)
-    final_args = (lambda to: sendf.at[to], recvf, sf, rf)
-    for i in range(1, NBAND):
-        band_copy(i, *final_args).start()
-    recvf[pl.ds(band, 1)] = sendf[pl.ds(band, 1)]
-
+    couple(me, hsub, factor, factor_wide, y_own, z_buf, sendz, sendr)
+    z_args = (lambda to: sendz.at[to], recvz, sz, rz)
+    row_args = (lambda to: sendr, recvr, sr, rr)
+    for i in range(1, NBAND):
+        band_copy(i, *z_args).start()
+    for i in range(1, NBAND):
+        band_copy(i, *row_args).start()
+    recvz[pl.ds(band, 1)] = sendz[pl.ds(band, 1)]
+    recvr[pl.ds(band, 1)] = sendr[...].reshape(1, 8, ORDER)
+
+    vector_weights(basis, y_own, w_buf, bands_part)
+    bands_args = (lambda to: bands_part.at[to], recvb, sb, rb)
+    for i in range(1, NBAND):
+        band_copy(i, *bands_args).start()
+    recvb[pl.ds(band, 1)] = bands_part[pl.ds(band, 1)]
     for i in range(1, NBAND):
         band_arrival(i, *new_args).wait_recv()
     slot = lax.broadcasted_iota(jnp.int32, (16, 128), 1) & (NZC - 1)
@@ -565,11 +569,16 @@
         device_id_type=MESH,
     )
     recv3[pl.ds(own, 1)] = send3[pl.ds(own, 1)]
-    vector_weights(basis, y_own, w_buf, bands_part)
-    bands_args = (lambda to: bands_part.at[to], recvb, sb, rb)
-    for i in range(1, NBAND):
-        band_copy(i, *bands_args).start()
-    recvb[pl.ds(band, 1)] = bands_part[pl.ds(band, 1)]
+    for i in range(1, NBAND):
+        band_arrival(i, *z_args).wait_recv()
+    z_sum = recvz[0] + recvz[1] + recvz[2] + recvz[3]
+    old = dot_nt(z_sum.astype(BF16), factor[...].astype(BF16))
+    sendf[...] = old.reshape(NBAND, 8, ORDER)
+    final_args = (lambda to: sendf.at[to], recvf, sf, rf)
+    for i in range(1, NBAND):
+        band_copy(i, *final_args).start()
+    recvf[pl.ds(band, 1)] = sendf[pl.ds(band, 1)]
+
     hblock_out[...] = hall[pl.ds(band, 1)].reshape(32, 128)
     for i in range(1, NBAND):
         band_arrival(i, *bands_args).wait_recv()
@@ -580,13 +589,18 @@
     for i in range(1, NBAND):
         band_arrival(i, *final_args).wait_recv()
     old_part = recvf[0] + recvf[1] + recvf[2] + recvf[3]
-    wide_rows = jnp.concatenate([rows[32:40, :]] * 4 + [jnp.zeros((96, ORDER), F32)], 0).astype(BF16)
+    for i in range(1, NBAND):
+        band_arrival(i, *row_args).wait_recv()
+    new_rows = jnp.concatenate([recvr[b, 6:8, :] for b in range(NBAND)], 0)
+    wide_rows = jnp.concatenate([new_rows] * 4 + [jnp.zeros((96, ORDER), F32)], 0).astype(BF16)
     fft_wait_send(*first)
     back_all.wait_send()
     for i in range(1, NBAND):
         band_copy(i, *bands_args).wait_send()
         band_copy(i, *new_args).wait_send()
         band_copy(i, *final_args).wait_send()
+        band_copy(i, *z_args).wait_send()
+        band_copy(i, *row_args).wait_send()
 
     sum_all.wait_recv()
     total = jnp.sum(recv3[...].reshape(NBAND * NFFT, 128), axis=0, keepdims=True)
@@ -613,13 +627,16 @@
         scratch_shapes=[pltpu.VMEM(x.shape, x.dtype) for x in operands]
         + [
             pltpu.VMEM((2, 16, TILE, 128), F32),
+            pltpu.VMEM((2, TILE, 256), F32),
             pltpu.VMEM((2, 8 * ROUNDS, TILE, 128), F32),
-            pltpu.VMEM((ORDER, ORDER), BF16),
             pltpu.VMEM((ORDER, 128), F32),
             pltpu.VMEM((128, ORDER), BF16),
             pltpu.VMEM((40, GROUP), F32),
             pltpu.VMEM((ORDER, 128), F32),
-            pltpu.VMEM((40, ORDER), F32),
+            pltpu.VMEM((NBAND, 32, GROUP), F32),
+            pltpu.VMEM((NBAND, 32, GROUP), F32),
+            pltpu.VMEM((8, ORDER), F32),
+            pltpu.VMEM((NBAND, 8, ORDER), F32),
             pltpu.VMEM((128, 2048), BF16),
             pltpu.VMEM((NBAND, 32, 128), BF16),
             pltpu.VMEM((NFFT, 8, 128), F32),
@@ -650,7 +667,7 @@
             pltpu.VMEM((8, 16, 128), F32),
         ]
         + [dma] * 6
-        + [dma((NBAND,))] * 6
+        + [dma((NBAND,))] * 10
         + [dma((len(operands),))],
         compiler_params=pltpu.CompilerParams(
             collective_id=0, has_side_effects=True, vmem_limit_bytes=56 * 2**20

time: 34.9 us -> 34.3 us (0.983)
  Pallas kernels: 33.9 us -> 33.5 us
    pallas_call x1, Pallas kernels: 32.1 us -> 31.6 us  [main_part(): pl.pallas_call(main_kernel, out_shape=(jax.ShapeDtypeStruct((32, 128), BF...]
where the time goes in v7:
time: 34.3 us; the launch traced here: 34.2 us
  Pallas kernels  33.5 us (98%)
  between operations  0.64 us (2%)
    pallas_call x1, Pallas kernels, main_part(): pl.pallas_call(main_kernel, out_shape=(jax.ShapeDtypeStruct((32, 128), BF...  31.6 us
    pallas_call x1, Pallas kernels, result_part(): pl.pallas_call(result_kernel, out_shape=tuple((jax.ShapeDtypeStruct(x.sha...  1.88 us

profile of v7, /device:TPU:1, one launch (start us, length us, event | category | flops | bytes accessed | tf_op | source)
XLA Modules:
  0.0 34.2 jit_solution(6475257837048236072)
XLA Ops:
  0.6 31.6 %main_part.1 = (bf16[32,128]{1,0:T(8,128)(2,1)}, f32[4,512]{1,0:T(4,128)}, bf16[32,128]{1,0:T(8,128)(2,1)}) custom-call(bf16[2048,128]{1,0:T(8,128)(2,1)} %bitcast.6, s32[1,512]{1,0:T(1,128)} %bitcast.9, f32[240,32]{1,0:T(8,128)} %bitcast.8, bf16[256,256]{1,0:T(8,128)(2,1)} %constant.10.clone.tz_in, f32[512,512]{1,0:T(8,128)} %inv_in.1, f32[504,128]{1,0:T(8,128)} %bitcast.7, ...), custom_call_target="tpu_custom_call" | custom-call | tf_op jit(solution)/shard_map/main_part/pallas_call | solution.py:618
  32.3 1.9 %result_part.1 = (bf16[32,128]{1,0:T(8,128)(2,1)}, f32[4,512]{1,0:T(4,128)}, bf16[32,128]{1,0:T(8,128)(2,1)}) custom-call(bf16[32,128]{1,0:T(8,128)(2,1)} %get-tuple-element.9.refs_0_, f32[4,512]{1,0:T(4,128)} %get-tuple-element.10.refs_1_, bf16[32,128]{1,0:T(8,128)(2,1)} %get-tuple-element.11.refs_2_), custom_call_target="tpu_custom_call" | custom-call | tf_op jit(solution)/shard_map/result_part/pallas_call | solution.py:692

commit v8 on v7

--- a/solution.py
+++ b/solution.py
@@ -231,9 +231,9 @@
 
 
 def main_kernel(
-    basis_in, columns_in, angles_in, tz_in, inv_in, hsub_in, tx_in, ty_in, ty_t_in, potential_in, tb_in,
+    basis_in, columns_in, angles_in, inv_in, hsub_in, tx_in, ty_in, ty_t_in, potential_in, tb_in,
     hblock_out, rotated_out, bands_out,
-    basis, columns, angles, tz, inv, hsub, tx, ty, ty_t, potential, tb,
+    basis, columns, angles, inv, hsub, tx, ty, ty_t, potential, tb,
     state, turned, table, factor, factor_wide, y_own, z_buf, sendz, recvz, sendr, recvr, w_buf, bands_part,
     send1, recv1, send2, recv2, send3, recv3, new_own, news, hall, recvb, sendf, recvf,
     q_buf, u_buf, a_cos, a_sin, phase, phase_out, folded, right1, right2, radius, coef, d_buf, p_buf, g_buf,
@@ -243,8 +243,8 @@
     me = lax.axis_index("fft")
 
     inputs = (
-        (basis_in, basis), (tz_in, tz), (angles_in, angles), (columns_in, columns), (tx_in, tx),
-        (ty_in, ty), (ty_t_in, ty_t), (inv_in, inv), (potential_in, potential), (tb_in, tb), (hsub_in, hsub),
+        (basis_in, basis), (tb_in, tb), (angles_in, angles), (columns_in, columns), (tx_in, tx),
+        (ty_in, ty), (ty_t_in, ty_t), (inv_in, inv), (potential_in, potential), (hsub_in, hsub),
     )
     copies = [pltpu.make_async_copy(a, b, loads.at[i]) for i, (a, b) in enumerate(inputs)]
     copies[0].start()
@@ -273,8 +273,8 @@
         for steps in near:
             to = peer(steps)
             pltpu.make_async_remote_copy(
-                src_ref=send if whole else send.at[to[1]],
-                dst_ref=recv.at[me],
+                src_ref=send.at[to[1], pl.ds(0, 3)],
+                dst_ref=recv.at[me, pl.ds(0, 3)],
                 send_sem=ssem,
                 recv_sem=rsem,
                 device_id=to,
@@ -282,7 +282,7 @@
             ).start()
 
     def fft_all(send, recv, ssem, rsem, whole):
-        part = recv.at[pl.ds(0, NFFT - 1)]
+        part = recv.at[pl.ds(0, NFFT - 1), pl.ds(0, 3)]
         return pltpu.make_async_remote_copy(
             src_ref=part,
             dst_ref=part,
@@ -330,11 +330,16 @@
             jnp.concatenate([none, new[0:16]], 1),
             jnp.concatenate([new[16:32], none], 1),
             jnp.concatenate([none, new[16:32]], 1),
-            jnp.zeros((64, 256), BF16),
         ],
         0,
     )
-    send1[...] = dot_nt(tz[...], right).reshape(NFFT, 8, 128)
+    blank = jnp.zeros((64, 256), BF16)
+    right = jnp.concatenate(
+        [jnp.concatenate([right, blank], 1), jnp.concatenate([blank, right], 1)], 0
+    )
+    pencils = dot_nt(tb[...], right)
+    for r in range(3):
+        send1[:, r, :] = pencils[NFFT * r : NFFT * r + NFFT]
     first = (send1, recv1, s1, r1, False)
     pl.semaphore_wait(barrier, NFFT - 1 + NBAND - 1)
     fft_start(*first)
@@ -380,27 +385,29 @@
     radius[...] = jnp.broadcast_to(freq_x * freq_x + freq_y * freq_y, (128, NCOL)).T
     g_buf[...] = jnp.zeros_like(g_buf)
 
-    for i in range(7, 11):
+    for i in range(7, 10):
         copies[i].wait()
     fold_potential(potential, folded)
     fft_wait_recv(*first)
 
     lanes = lax.broadcasted_iota(jnp.int32, (8, 128), 1)
-    for q in range(4):
-        for j in range(4):
-            total = jnp.zeros((8, 128), F32)
-            for t in range(8):
-                piece = recv1[8 * j + t]
-                move = (16 * t - 16 * q) % 128
-                if move:
-                    piece = pltpu.roll(piece, move, 1)
-                total = jnp.where((lanes >> 4) == t, piece, total)
-            coef[q, :, 128 * j : 128 * j + 128] = total
+    wide_lanes = lax.broadcasted_iota(jnp.int32, (16, 128), 1)
+    lines = [jnp.concatenate([recv1[8 * j + t] for j in range(4)], 0) for t in range(8)]
+    for q in range(8):
+        total = jnp.zeros((16, 128), F32)
+        for t in range(8):
+            piece = lines[t]
+            move = (16 * t - 16 * q) % 128
+            if move:
+                piece = pltpu.roll(piece, move, 1)
+            total = jnp.where((wide_lanes >> 4) == t, piece, total)
+        coef[q] = total
 
     def mix(v):
-        old_re, old_im = coef[2 * v], coef[2 * v + 1]
-        coef[2 * v] = old_re * phase[0] - old_im * phase[1]
-        coef[2 * v + 1] = old_re * phase[1] + old_im * phase[0]
+        for q in (2 * v, 2 * v + 4):
+            old_re, old_im = coef[q], coef[q + 1]
+            coef[q] = old_re * phase_out[0] - old_im * phase_out[1]
+            coef[q + 1] = old_re * phase_out[1] + old_im * phase_out[0]
 
     def unmix(v):
         for q in (2 * v, 2 * v + 4):
@@ -415,9 +422,13 @@
         return pl.ds(4 * HALF * z, 4 * HALF)
 
     def spread(v, z):
-        for a, part in enumerate((a_cos, a_sin)):
-            for i in range(2):
-                d_buf[block(z, a, i), :] = (part[...] * coef[2 * v + i, z : z + 1, :]).astype(BF16)
+        for i in range(2):
+            q = 4 * (z % 2) + 2 * v + i
+            row = jnp.concatenate(
+                [coef[q, 4 * j + z // 2 : 4 * j + z // 2 + 1, :] for j in range(4)], 1
+            )
+            for a, part in enumerate((a_cos, a_sin)):
+                d_buf[block(z, a, i), :] = (part[...] * row).astype(BF16)
 
     def to_field(v, z):
         q_buf[plane(z), :] = dot(d_buf[plane(z), :], right1[...])
@@ -460,7 +471,6 @@
         unmix(v)
 
     volume = 1.0 / float(NG) ** 3
-    wide_lanes = lax.broadcasted_iota(jnp.int32, (16, 128), 1)
     for t in range(8):
         total = jnp.zeros((16, 128), F32)
         for q in range(8):
@@ -639,8 +649,8 @@
             pltpu.VMEM((NBAND, 8, ORDER), F32),
             pltpu.VMEM((128, 2048), BF16),
             pltpu.VMEM((NBAND, 32, 128), BF16),
-            pltpu.VMEM((NFFT, 8, 128), F32),
-            pltpu.VMEM((NFFT, 8, 128), F32),
+            pltpu.VMEM((NFFT, 4, 128), F32),
+            pltpu.VMEM((NFFT, 4, 128), F32),
             pltpu.VMEM((NFFT, 4, 128), F32),
             pltpu.VMEM((NBAND * NFFT, 4, 128), F32),
             pltpu.VMEM((NBAND * NFFT, 1, 128), F32),
@@ -661,7 +671,7 @@
             pltpu.VMEM((NCOL, 256), BF16),
             pltpu.VMEM((256, NCOL), BF16),
             pltpu.VMEM((NCOL, 128), F32),
-            pltpu.VMEM((4, 8, NCOL), F32),
+            pltpu.VMEM((8, 16, 128), F32),
             pltpu.VMEM((4 * SLAB * HALF, NCOL), BF16),
             pltpu.VMEM((4 * SLAB * HALF, 256), BF16),
             pltpu.VMEM((8, 16, 128), F32),
@@ -706,7 +716,6 @@
         basis.reshape(2048, 128),
         colmap.reshape(1, NCOL),
         angles.reshape(8 * ROUNDS, TILE),
-        jnp.asarray(z_table().astype(BF16)),
         inv_factor,
         hsub_old.T,
         jnp.asarray(x_table()),

time: 34.3 us -> 34 us (level)
  no operation moved by 1% of the time
where the time goes in v8:
time: 34 us; the launch traced here: 33.9 us
  Pallas kernels  33.3 us (98%)
  between operations  0.64 us (2%)
    pallas_call x1, Pallas kernels, main_part(): pl.pallas_call(main_kernel, out_shape=(jax.ShapeDtypeStruct((32, 128), BF...  31.4 us
    pallas_call x1, Pallas kernels, result_part(): pl.pallas_call(result_kernel, out_shape=tuple((jax.ShapeDtypeStruct(x.sha...  1.88 us

profile of v8, /device:TPU:1, one launch (start us, length us, event | category | flops | bytes accessed | tf_op | source)
XLA Modules:
  0.0 33.9 jit_solution(11603805860548217906)
XLA Ops:
  0.6 31.4 %main_part.1 = (bf16[32,128]{1,0:T(8,128)(2,1)}, f32[4,512]{1,0:T(4,128)}, bf16[32,128]{1,0:T(8,128)(2,1)}) custom-call(bf16[2048,128]{1,0:T(8,128)(2,1)} %bitcast.6, s32[1,512]{1,0:T(1,128)} %bitcast.9, f32[240,32]{1,0:T(8,128)} %bitcast.8, f32[512,512]{1,0:T(8,128)} %inv_in.1, f32[504,128]{1,0:T(8,128)} %bitcast.7, bf16[192,512]{1,0:T(8,128)(2,1)} %constant.8.clone.tx_in, ...), custom_call_target="tpu_custom_call" | custom-call | tf_op jit(solution)/shard_map/main_part/pallas_call | solution.py:628
  32.0 1.9 %result_part.1 = (bf16[32,128]{1,0:T(8,128)(2,1)}, f32[4,512]{1,0:T(4,128)}, bf16[32,128]{1,0:T(8,128)(2,1)}) custom-call(bf16[32,128]{1,0:T(8,128)(2,1)} %get-tuple-element.9.refs_0_, f32[4,512]{1,0:T(4,128)} %get-tuple-element.10.refs_1_, bf16[32,128]{1,0:T(8,128)(2,1)} %get-tuple-element.11.refs_2_), custom_call_target="tpu_custom_call" | custom-call | tf_op jit(solution)/shard_map/result_part/pallas_call | solution.py:702
